TPU v7x, 256 devices: a whole 4x4x8 slice. The times are simulated.
256 devices in a mesh: grp: 4 (over z_lo), seq: 64 (over y, z_hi, x, core).
Axes of the slice: x: 4, y: 4, z: 8 (z_hi: 2, z_lo: 4; z = z_hi * 4 + z_lo), core: 2. Of those that a mesh axis runs over, the one named last changes fastest.
Arguments:
- tokens: bfloat16 [64, 1024, 1024], P('seq', 'grp'), may hold values from -6 to 6
- lengths: int32 [64, 3], P('seq'), may hold values from 1 to 768, 1024 in all within a row
- in_gain: float32 [1024], replicated, may hold values from 0.25 to 1.75
- out_gain: float32 [1024], replicated, may hold values from 0.25 to 1.75
- w_in: bfloat16 [1024, 2560], replicated, may hold values from -0.1875 to 0.1875
- w_out: bfloat16 [1024, 1024], replicated, may hold values from -0.1875 to 0.1875
- w_qgate: float32 [1024, 8], replicated, may hold values from -0.1875 to 0.1875
- w_xgate: float32 [1024, 8], replicated, may hold values from -0.1875 to 0.1875
- item_table: bfloat16 [32768, 1024], P('seq'), may hold values from -6 to 6
- neg_owner: int32 [64, 2048, 1], P('seq', 'grp'), may hold values from 0 to 63; in each aligned block of 512 rows (0 to 511, 512 to 1023, ..., all dimensions but the last counted through in order) at most 16 rows name the same one
- neg_slot: int32 [64, 2048], P('seq', 'grp'), may hold values from 0 to 511
- pos_owner: int32 [64, 1024, 1], P('seq', 'grp'), may hold values from 0 to 63; in each aligned block of 256 rows (0 to 255, 256 to 511, ..., all dimensions but the last counted through in order) at most 8 rows name the same one
- pos_slot: int32 [64, 1024], P('seq', 'grp'), may hold values from 0 to 511
Outputs:
- losses: float32 [64, 1024], P('seq', 'grp')
- query_grad: bfloat16 [64, 1024, 1024], P('seq', 'grp')
- table_grad: float32 [32768, 1024], P('seq')
Inputs may be any that keep to these rules, and one draw needn't show every extreme that they name: `neg_owner`: in the 512 rows of one device no owner is named more than 16 times, a bound that some block reaches. `pos_owner`: in the 256 rows of one device no owner is named more than 8 times, a bound that some block reaches. `lengths`: each row sums to 1024; its largest is exactly 768.
All inputs are finite; a program needn't handle non-finite values.
Results may differ from a plain program's by a relative error of at most 0.014.
Values may be sent and summed in bfloat16 or wider, within the bound.
No kernel may reach another device: no remote copies, remote signals or barrier semaphores. Data moves between devices by JAX's collectives and lax.ppermute only.
A program may use at most 128 MiB of HBM per device.

v0:
```python
import math

import jax
import jax.numpy as jnp
from jax import lax
from jax.sharding import PartitionSpec as P

HEADS = 4
PARTS_SIZE = 8


INV_TEMP = 32.0
GATE_SCALE = 2.0


def from_behind(value, axis, steps):
    count = lax.axis_size(axis)
    initial, last = (max(0, -steps), min(count, count - steps))
    return lax.ppermute(value, axis, [(source, source + steps) for source in range(initial, last)])


def layer_norm(values, gain_vec):
    average = jnp.mean(values, -1, keepdims=True)
    centred = values - average
    spread = jnp.mean(centred * centred, -1, keepdims=True)
    return centred * lax.rsqrt(spread + 1e-05) * gain_vec


def segment_of(positions, lengths):
    seq_ends = jnp.cumsum(lengths)
    return jnp.sum((seq_ends[None, :] <= positions[:, None]).astype(jnp.int32), 1)


def trunk_front(block_tokens, in_gain, w_in):
    normed = layer_norm(block_tokens.astype(jnp.float32), in_gain).astype(jnp.bfloat16)
    projected = jax.nn.silu(jnp.dot(normed, w_in, preferred_element_type=jnp.float32)).astype(
        jnp.bfloat16
    )
    model_width = block_tokens.shape[1]
    qk_width = (w_in.shape[1] - 2 * model_width) // 2
    return (
        projected[:, :model_width],
        projected[:, model_width : 2 * model_width],
        projected[:, 2 * model_width : 2 * model_width + qk_width],
        projected[:, 2 * model_width + qk_width :],
    )


def attend(queries, keys_all, values_all, query_pos, key_pos, lengths):
    query_seg = segment_of(query_pos, lengths)
    key_seg = segment_of(key_pos, lengths)
    visible = (
        (query_seg[:, None] == key_seg[None, :])
        & (key_pos[None, :] <= query_pos[:, None])
        & (key_pos[None, :] >= 0)
    )
    q_heads = queries.reshape(queries.shape[0], HEADS, -1)
    k_heads = keys_all.reshape(keys_all.shape[0], HEADS, -1)
    v_heads = values_all.reshape(values_all.shape[0], HEADS, -1)
    head_size = q_heads.shape[2]
    scores = jnp.einsum("ihd,jhd->hij", q_heads, k_heads, preferred_element_type=jnp.float32) * (
        1.0 / math.sqrt(head_size)
    )
    weights = (jax.nn.silu(scores) * visible[None].astype(jnp.float32)).astype(jnp.bfloat16)
    mixed = jnp.einsum("hij,jhd->ihd", weights, v_heads, preferred_element_type=jnp.float32)
    return mixed.reshape(queries.shape[0], -1)


def trunk_back(block_tokens, gate_part, mixed, out_gain, w_out):
    gated = (layer_norm(mixed, out_gain) * gate_part.astype(jnp.float32)).astype(jnp.bfloat16)
    return block_tokens.astype(jnp.float32) + jnp.dot(
        gated, w_out, preferred_element_type=jnp.float32
    )


def unit_parts(matrix_rows):
    pieces = matrix_rows.reshape(matrix_rows.shape[0], PARTS_SIZE, -1)
    return pieces * lax.rsqrt(jnp.sum(pieces * pieces, -1, keepdims=True) + 1e-06)


def gate_weights(logits):
    raised = jnp.exp(GATE_SCALE * jnp.tanh(logits))
    return raised / jnp.sum(raised, 0, keepdims=True)


def block_loss(query, neg_rows, pos_rows, w_qgate, w_xgate):
    highest = lax.Precision.HIGHEST
    query_unit = unit_parts(query)
    neg_unit = unit_parts(neg_rows)
    pos_unit = unit_parts(pos_rows)
    query_gate = jnp.dot(query, w_qgate, precision=highest).T
    neg_gate = jnp.dot(neg_rows, w_xgate, precision=highest).T
    pos_gate = jnp.dot(pos_rows, w_xgate, precision=highest).T
    neg_cos = jnp.einsum("ipd,xpd->pix", query_unit, neg_unit, precision=highest)
    neg_mix = gate_weights(query_gate[:, :, None] + neg_gate[:, None, :])
    neg_logit = INV_TEMP * jnp.sum(neg_mix * neg_cos, 0)
    pos_cos = jnp.sum(query_unit * pos_unit, -1).T
    pos_mix = gate_weights(query_gate + pos_gate)
    pos_logit = INV_TEMP * jnp.sum(pos_mix * pos_cos, 0)
    partition = jnp.exp(pos_logit) + jnp.sum(jnp.exp(neg_logit), -1)
    return jnp.log(partition) - pos_logit


def pack_slots(owner_ids, slot_ids, capacity, owners):
    marks = (owner_ids[:, None] == jnp.arange(owners, dtype=jnp.int32)[None, :]).astype(jnp.int32)
    rank_in = jnp.sum((jnp.cumsum(marks, 0) - marks) * marks, 1)
    place = owner_ids * capacity + rank_in
    buffer = jnp.full((owners * capacity,), -1, jnp.int32).at[place].set(slot_ids)
    return (buffer.reshape(owners, capacity), place)


def fetch_items(item_table, neg_owner, neg_slot, pos_owner, pos_slot, neg_cap, pos_cap, owners):
    model_width = item_table.shape[1]
    neg_buffer, neg_place = pack_slots(neg_owner, neg_slot, neg_cap, owners)
    pos_buffer, pos_place = pack_slots(pos_owner, pos_slot, pos_cap, owners)
    wanted = jnp.concatenate([neg_buffer, pos_buffer], 1)
    arrived = lax.all_to_all(wanted, "seq", split_axis=0, concat_axis=0, tiled=True)
    looked = jnp.where(
        (arrived >= 0)[..., None], item_table[jnp.maximum(arrived, 0)], jnp.zeros((), jnp.bfloat16)
    )
    returned = lax.all_to_all(looked, "seq", split_axis=0, concat_axis=0, tiled=True)
    neg_rows = returned[:, :neg_cap].reshape(-1, model_width)[neg_place]
    pos_rows = returned[:, neg_cap:].reshape(-1, model_width)[pos_place]
    return (neg_rows, pos_rows, arrived, neg_place, pos_place)


def local(
    tokens,
    lengths,
    in_gain,
    out_gain,
    w_in,
    w_out,
    w_qgate,
    w_xgate,
    item_table,
    neg_owner,
    neg_slot,
    pos_owner,
    pos_slot,
):
    own_tokens = tokens[0]
    own_lengths = lengths[0]
    local_rows = own_tokens.shape[0]
    model_width = own_tokens.shape[1]
    owners = lax.axis_size("seq")
    reach = lax.axis_size("grp") - 1
    neg_owner_ids = neg_owner[0, :, 0]
    neg_slot_ids = neg_slot[0]
    pos_owner_ids = pos_owner[0, :, 0]
    pos_slot_ids = pos_slot[0]
    neg_cap = max(2, 2 * neg_slot_ids.shape[0] // owners)
    pos_cap = max(2, 2 * local_rows // owners)
    gate_part, value_part, query_part, key_part = trunk_front(own_tokens, in_gain, w_in)
    start = lax.axis_index("grp") * local_rows
    key_list = [key_part]
    value_list = [value_part]
    moving = (key_part, value_part)
    for hop_count in range(reach):
        moving = from_behind((moving[0], moving[1]), "grp", 1)
        key_list.insert(0, moving[0])
        value_list.insert(0, moving[1])
    query_pos = start + jnp.arange(local_rows, dtype=jnp.int32)
    key_pos = start - reach * local_rows + jnp.arange((reach + 1) * local_rows, dtype=jnp.int32)
    mixed = attend(
        query_part,
        jnp.concatenate(key_list, 0),
        jnp.concatenate(value_list, 0),
        query_pos,
        key_pos,
        own_lengths,
    )
    query = trunk_back(own_tokens, gate_part, mixed, out_gain, w_out)
    neg_rows, pos_rows, arrived, neg_place, pos_place = fetch_items(
        item_table,
        neg_owner_ids,
        neg_slot_ids,
        pos_owner_ids,
        pos_slot_ids,
        neg_cap,
        pos_cap,
        owners,
    )

    def loss_of(query_in, neg_in, pos_in):
        return block_loss(query_in, neg_in, pos_in, w_qgate, w_xgate)

    losses, pullback = jax.vjp(
        loss_of, query, neg_rows.astype(jnp.float32), pos_rows.astype(jnp.float32)
    )
    query_back, neg_back, pos_back = pullback(jnp.ones_like(losses))
    neg_grads = (
        jnp.zeros((owners * neg_cap, model_width), jnp.float32)
        .at[neg_place]
        .set(neg_back)
        .reshape(owners, neg_cap, model_width)
    )
    pos_grads = (
        jnp.zeros((owners * pos_cap, model_width), jnp.float32)
        .at[pos_place]
        .set(pos_back)
        .reshape(owners, pos_cap, model_width)
    )
    owner_grads = lax.all_to_all(
        jnp.concatenate([neg_grads, pos_grads], 1).astype(jnp.bfloat16),
        "seq",
        split_axis=0,
        concat_axis=0,
        tiled=True,
    ).astype(jnp.float32)
    table_part = (
        jnp.zeros((item_table.shape[0], model_width), jnp.float32)
        .at[jnp.maximum(arrived, 0).reshape(-1)]
        .add(owner_grads.reshape(-1, model_width))
    )
    table_grad = lax.psum(table_part.astype(jnp.bfloat16), "grp").astype(jnp.float32)
    return (losses[None], query_back.astype(jnp.bfloat16)[None], table_grad)


def solution(mesh):
    in_specs = (
        P("seq", "grp", None),
        P("seq", None),
        P(),
        P(),
        P(),
        P(),
        P(),
        P(),
        P("seq", None),
        P("seq", "grp", None),
        P("seq", "grp"),
        P("seq", "grp", None),
        P("seq", "grp"),
    )
    out_specs = (P("seq", "grp"), P("seq", "grp", None), P("seq", None))
    return jax.shard_map(local, mesh=mesh, in_specs=in_specs, out_specs=out_specs, check_vma=False)
```

profile of v0, /device:TPU:4, one launch (start us, length us, event | category | flops | bytes accessed | tf_op | source)
XLA Modules:
  0.0 443.1 jit_solution(4980725063261622228)
XLA Ops:
  15.7 2.6 scatter_custom_fusion
  18.4 24.5 %all_to_all.19 = s32[64,1,24]{2,1,0:T(1,128)S(1)} all-to-all(s32[64,1,24]{2,1,0:T(1,128)S(1)} %bitcast.200), channel_id=1, replica_groups=mesh['grp'=4,'seq'=64] {'seq'}, dimensions={0} | all-to-all | bytes 12288 | tf_op jit(solution)/shard_map/all_to_all | solution.py:117
  43.3 5.8 %gather_fusion = bf16[1536,1024]{1,0:T(8,128)(2,1)} fusion(bf16[512,1024]{1,0:T(8,128)(2,1)S(1)} %copy-done.2, s32[2048]{0:T(1024)S(1)} %pad_clamp_fusion), kind=kCustom, calls=%fused_computation | custom fusion | bytes 6297600 | tf_op jit(solution)/shard_map/gather | solution.py:119
  49.1 3.3 broadcast_select_fusion
  52.4 7.4 %all-to-all-start.1 = ((bf16[64,24,1024]{2,1,0:T(8,128)(2,1)}), bf16[64,24,1024]{2,1,0:T(8,128)(2,1)}, u32[]{:S(2)}, u32[]{:S(2)}) async-start(bf16[64,24,1024]{2,1,0:T(8,128)(2,1)} %broadcast_select_fusion), calls=%async_computation.1 | async-start | bytes 6291456 | tf_op jit(solution)/shard_map/all_to_all | solution.py:121
  60.4 4.2 multiply_convert_fusion.1
  64.7 3.7 collective-permute-start
  70.8 68.7 %collective-permute-done = bf16[256,1024]{1,0:T(8,128)(2,1)} collective-permute-done((bf16[256,1024]{1,0:T(8,128)(2,1)S(1)}, bf16[256,1024]{1,0:T(8,128)(2,1)}, u32[]{:S(2)}, u32[]{:S(2)}) %collective-permute-start) | collective-permute-done | bytes 524320 | tf_op jit(solution)/shard_map/ppermute | solution.py:19
  139.4 5.3 %collective-permute-start.1 = (bf16[256,1024]{1,0:T(8,128)(2,1)}, bf16[256,1024]{1,0:T(8,128)(2,1)}, u32[]{:S(2)}, u32[]{:S(2)}) collective-permute-start(bf16[256,1024]{1,0:T(8,128)(2,1)} %collective-permute-done), channel_id=1, source_target_pairs={{0,64},{64,128},{128,192},{1,65},{65,129},{129,193},{2,66},{66,130... | collective-permute-start | bytes 1572872 | tf_op jit(solution)/shard_map/ppermute | solution.py:19
  146.9 9.2 %collective-permute-done.1 = bf16[256,1024]{1,0:T(8,128)(2,1)} collective-permute-done((bf16[256,1024]{1,0:T(8,128)(2,1)}, bf16[256,1024]{1,0:T(8,128)(2,1)}, u32[]{:S(2)}, u32[]{:S(2)}) %collective-permute-start.1) | collective-permute-done | bytes 524320 | tf_op jit(solution)/shard_map/ppermute | solution.py:19
  156.1 5.2 %collective-permute-start.2 = (bf16[256,1024]{1,0:T(8,128)(2,1)}, bf16[256,1024]{1,0:T(8,128)(2,1)}, u32[]{:S(2)}, u32[]{:S(2)}) collective-permute-start(bf16[256,1024]{1,0:T(8,128)(2,1)} %collective-permute-done.1), channel_id=1, source_target_pairs={{0,64},{64,128},{128,192},{1,65},{65,129},{129,193},{2,66},{66,130... | collective-permute-start | bytes 1572872 | tf_op jit(solution)/shard_map/ppermute | solution.py:19
  162.6 3.2 collective-permute-start.5
  166.5 5.3 %collective-permute-done.5 = bf16[256,256]{1,0:T(8,128)(2,1)} collective-permute-done((bf16[256,256]{1,0:T(8,128)(2,1)S(1)}, bf16[256,256]{1,0:T(8,128)(2,1)}, u32[]{:S(2)}, u32[]{:S(2)}) %collective-permute-start.5) | collective-permute-done | bytes 131104 | tf_op jit(solution)/shard_map/ppermute | solution.py:19
  173.8 2.8 pad_maximum_fusion.1
  176.6 4.0 copy.197
  180.6 4.2 fusion.84
  198.2 2.8 gather_fusion.2
  208.2 4.6 %multiply_reduce_fusion.1 = (f32[256,512]{1,0:T(8,128)S(1)}, f32[8,256,512]{2,1,0:T(8,128)S(1)}) fusion(f32[256,512]{1,0:T(8,128)S(1)} %fusion.3, f32[8,512]{1,0:T(8,128)S(1)} %convolution_bitcast_fusion, f32[8,256]{1,0:T(8,128)S(1)} %bitcast.195, f32[512,8,128]{0,2,1:T(8,128)S(1)} %bitcast.175, f32[512,8]{0,1:T(8,128)S(1)} %add_rsqrt_fusion, ...), kind=kOutput, calls=%fused_computation.12 | convolution fusion | flops 1616510976 | bytes 8437760 | tf_op jit(solution)/shard_map/jvp(ipd,xpd->pix)/dot_general | solution.py:94
  213.3 5.1 %fusion.8 = (f32[512,8]{0,1:T(8,128)S(1)}, f32[8,512,128]{1,2,0:T(8,128)}) fusion(f32[512,1024]{0,1:T(8,128)S(1)} %copy.183, f32[256,8,128]{0,2,1:T(8,128)S(1)} %copy-done.3, f32[256,8]{0,1:T(8,128)S(1)} %get-tuple-element.23, f32[256,512]{1,0:T(8,128)S(1)} %multiply_multiply_fusion.1, f32[256,512]{1,0:T(8,128)S(1)} %fusion.3, ...), kind=kOutput, calls=%fused_computation.29 | convolution fusion | flops 1616113664 | bytes 6340608 | tf_op jit(solution)/shard_map/transpose(jvp(ipd,xpd->pix))/dot_general | solution.py:94
  218.5 7.2 %multiply_reduce_fusion.3 = (f32[256,8]{0,1:T(8,128)S(1)}, f32[256,8]{0,1:T(8,128)S(1)}, f32[256,8,128]{0,2,1:T(8,128)}) fusion(f32[256,8,128]{0,2,1:T(8,128)S(1)} %copy-done.8, f32[256,8,128]{0,2,1:T(8,128)S(1)} %copy-done.3, f32[256,8]{0,1:T(8,128)S(1)} %divide_multiply_fusion, f32[256,8]{0,1:T(8,128)S(1)} %get-tuple-element.23, ...), kind=kOutput, calls=%fused_computation.65 | convolution fusion | flops 1617686528 | bytes 6373376 | tf_op jit(solution)/shard_map/transpose(jvp(ipd,xpd->pix))/dot_general | solution.py:94
  227.2 2.9 fusion.81
  234.9 2.5 copy.202
  238.5 2.5 copy.201
  241.4 4.3 convolution_add_fusion
  245.7 3.5 scatter_custom_fusion.3
  251.1 3.2 fusion.86
  256.2 3.2 copy.200
  259.4 5.6 %scatter_custom_fusion.2 = f32[1024,1024]{1,0:T(8,128)} fusion(s32[512]{0:T(512)S(1)} %bitcast.210, f32[512,1024]{1,0:T(8,128)S(1)} %copy-done.6, f32[512,1024]{1,0:T(8,128)} %copy.200, f32[]{:T(128)} %constant.21.clone.1), kind=kCustom, calls=%fused_computation.30 | custom fusion | flops 524288 | bytes 8388612 | tf_op jit(solution)/shard_map/scatter | solution.py:195
  268.0 54.9 %all_to_all.20 = bf16[64,24,1024]{2,1,0:T(8,128)(2,1)} all-to-all(bf16[64,24,1024]{2,1,0:T(8,128)(2,1)S(1)} %pad_maximum_fusion), channel_id=1, replica_groups=mesh['grp'=4,'seq'=64] {'seq'}, dimensions={0} | all-to-all | bytes 6291456 | tf_op jit(solution)/shard_map/all_to_all | solution.py:204
  322.8 14.5 %scatter_custom_fusion.4 = f32[512,1024]{1,0:T(8,128)S(1)} fusion(s32[1536]{0:T(1024)S(1)} %reshape.454, bf16[1536,1024]{1,0:T(8,128)(2,1)} %bitcast.178, f32[]{:T(128)} %constant.21.clone.1), kind=kCustom, calls=%fused_computation.8 | custom fusion | flops 3145728 | bytes 5242884 | tf_op jit(solution)/shard_map/scatter-add | solution.py:214
  345.1 88.3 %all-reduce.2.cloned.1.call-done = bf16[512,1024]{1,0:T(8,128)(2,1)} async-done(((bf16[512,1024]{1,0:T(8,128)(2,1)}), bf16[512,1024]{1,0:T(8,128)(2,1)}) %all-reduce.2.cloned.1.call-update) | async-done | bytes 1048592 | tf_op jit(solution)/shard_map/psum | solution.py:216
  433.3 2.8 convert_element_type.99
  (144 shorter events, 61.1 us)
Async XLA Ops:
  7.2 179.1 %copy-start = (bf16[1024,1024]{1,0:T(8,128)(2,1)S(1)}, bf16[1024,1024]{1,0:T(8,128)(2,1)}, u32[]{:S(2)}) copy-start(bf16[1024,1024]{1,0:T(8,128)(2,1)} %param.18) | copy-start | bytes 6291460
  7.2 36.1 %copy-start.2 = (bf16[512,1024]{1,0:T(8,128)(2,1)S(1)}, bf16[512,1024]{1,0:T(8,128)(2,1)}, u32[]{:S(2)}) copy-start(bf16[512,1024]{1,0:T(8,128)(2,1)} %param.21) | copy-start | bytes 3145732
  10.3 1.7 copy-start.14
  52.4 7.4 %copy-start.7 = (bf16[1,256,1024]{2,1,0:T(8,128)(2,1)S(1)}, bf16[1,256,1024]{2,1,0:T(8,128)(2,1)}, u32[]{:S(2)}) copy-start(bf16[1,256,1024]{2,1,0:T(8,128)(2,1)} %param.13) | copy-start | bytes 1572868
  52.4 7.9 %copy-start.17 = (f32[1024]{0:T(1024)S(1)}, f32[1024]{0:T(1024)}, u32[]{:S(2)}) copy-start(f32[1024]{0:T(1024)} %param.15) | copy-start | bytes 12292
  52.4 139.1 %all-to-all-start.1 = ((bf16[64,24,1024]{2,1,0:T(8,128)(2,1)}), bf16[64,24,1024]{2,1,0:T(8,128)(2,1)}, u32[]{:S(2)}, u32[]{:S(2)}) async-start(bf16[64,24,1024]{2,1,0:T(8,128)(2,1)} %broadcast_select_fusion), calls=%async_computation.1 | async-start | bytes 6291456 | tf_op jit(solution)/shard_map/all_to_all | solution.py:121
  59.8 373.5 %all-reduce.2.cloned.1.call-start = ((), (), s32[]{:S(2)}) async-start(), calls=%async_computation.3 | async-start | bytes 2097152 | tf_op jit(solution)/shard_map/psum | solution.py:216
  60.4 10.2 %copy-start.18 = (s32[1,3]{1,0:T(1,128)S(1)}, s32[1,3]{1,0:T(1,128)}, u32[]{:S(2)}) copy-start(s32[1,3]{1,0:T(1,128)} %param.14) | copy-start | bytes 40
  60.4 105.4 %copy-start.15 = (s32[256,1]{0,1:T(1,128)S(1)}, s32[256,1]{0,1:T(1,128)}, u32[]{:S(2)}) copy-start(s32[256,1]{0,1:T(1,128)} %copy-done.14) | copy-start | bytes 3076
  64.6 3.8 copy-start.10
  64.7 74.8 %collective-permute-start = (bf16[256,1024]{1,0:T(8,128)(2,1)S(1)}, bf16[256,1024]{1,0:T(8,128)(2,1)}, u32[]{:S(2)}, u32[]{:S(2)}) collective-permute-start(bf16[256,1024]{1,0:T(8,128)(2,1)S(1)} %slice.46), channel_id=1, source_target_pairs={{0,64},{64,128},{128,192},{1,65},{65,129},{129,193},{2,66},{66,130... | collective-permute-start | bytes 1572872 | tf_op jit(solution)/shard_map/ppermute | solution.py:19
  68.4 76.5 %collective-permute-start.3 = (bf16[256,256]{1,0:T(8,128)(2,1)S(1)}, bf16[256,256]{1,0:T(8,128)(2,1)S(1)}, u32[]{:S(2)}, u32[]{:S(2)}) collective-permute-start(bf16[256,256]{1,0:T(8,128)(2,1)S(1)} %get-tuple-element.11), channel_id=1, source_target_pairs={{0,64},{64,128},{128,192},{1,65},{65,129},{129,193},{2,66},{66,130... | collective-permute-start | bytes 393224 | tf_op jit(solution)/shard_map/ppermute | solution.py:19
  139.4 16.7 %collective-permute-start.1 = (bf16[256,1024]{1,0:T(8,128)(2,1)}, bf16[256,1024]{1,0:T(8,128)(2,1)}, u32[]{:S(2)}, u32[]{:S(2)}) collective-permute-start(bf16[256,1024]{1,0:T(8,128)(2,1)} %collective-permute-done), channel_id=1, source_target_pairs={{0,64},{64,128},{128,192},{1,65},{65,129},{129,193},{2,66},{66,130... | collective-permute-start | bytes 1572872 | tf_op jit(solution)/shard_map/ppermute | solution.py:19
  144.9 17.6 %collective-permute-start.4 = (bf16[256,256]{1,0:T(8,128)(2,1)S(1)}, bf16[256,256]{1,0:T(8,128)(2,1)S(1)}, u32[]{:S(2)}, u32[]{:S(2)}) collective-permute-start(bf16[256,256]{1,0:T(8,128)(2,1)S(1)} %collective-permute-done.3), channel_id=1, source_target_pairs={{0,64},{64,128},{128,192},{1,65},{65,129},{129,193},{2,66},{66,130... | collective-permute-start | bytes 393224 | tf_op jit(solution)/shard_map/ppermute | solution.py:19
  156.1 17.7 %collective-permute-start.2 = (bf16[256,1024]{1,0:T(8,128)(2,1)}, bf16[256,1024]{1,0:T(8,128)(2,1)}, u32[]{:S(2)}, u32[]{:S(2)}) collective-permute-start(bf16[256,1024]{1,0:T(8,128)(2,1)} %collective-permute-done.1), channel_id=1, source_target_pairs={{0,64},{64,128},{128,192},{1,65},{65,129},{129,193},{2,66},{66,130... | collective-permute-start | bytes 1572872 | tf_op jit(solution)/shard_map/ppermute | solution.py:19
  162.6 3.9 copy-start.13
  162.6 9.2 %collective-permute-start.5 = (bf16[256,256]{1,0:T(8,128)(2,1)S(1)}, bf16[256,256]{1,0:T(8,128)(2,1)}, u32[]{:S(2)}, u32[]{:S(2)}) collective-permute-start(bf16[256,256]{1,0:T(8,128)(2,1)S(1)} %collective-permute-done.4), channel_id=1, source_target_pairs={{0,64},{64,128},{128,192},{1,65},{65,129},{129,193},{2,66},{66,130... | collective-permute-start | bytes 393224 | tf_op jit(solution)/shard_map/ppermute | solution.py:19
  180.6 5.7 %copy-start.16 = (f32[1024]{0:T(1024)S(1)}, f32[1024]{0:T(1024)}, u32[]{:S(2)}) copy-start(f32[1024]{0:T(1024)} %param.16) | copy-start | bytes 12292
  186.3 4.3 copy-start.12
  194.2 2.1 copy-start.5
  198.2 4.5 %copy-start.11 = (f32[1024,8]{0,1:T(8,128)S(1)}, f32[1024,8]{0,1:T(8,128)}, u32[]{:S(2)}) copy-start(f32[1024,8]{0,1:T(8,128)} %param.20) | copy-start | bytes 98308
  202.8 5.4 %copy-start.3 = (f32[256,8,128]{0,2,1:T(8,128)S(1)}, f32[256,8,128]{0,2,1:T(8,128)}, u32[]{:S(2)}) copy-start(f32[256,8,128]{0,2,1:T(8,128)} %copy.180) | copy-start | bytes 3145732
  208.2 4.8 %copy-start.8 = (f32[256,8,128]{0,2,1:T(8,128)S(1)}, f32[256,8,128]{0,2,1:T(8,128)}, u32[]{:S(2)}) copy-start(f32[256,8,128]{0,2,1:T(8,128)} %copy.182) | copy-start | bytes 3145732
  249.2 5.1 %copy-start.9 = (f32[8,512,128]{1,2,0:T(8,128)S(1)}, f32[8,512,128]{1,2,0:T(8,128)}, u32[]{:S(2)}) copy-start(f32[8,512,128]{1,2,0:T(8,128)} %get-tuple-element.21) | copy-start | bytes 6291460
  256.2 3.2 copy-start.6
  322.8 15.7 %copy-start.4 = (f32[256,8,128]{0,2,1:T(8,128)S(1)}, f32[256,8,128]{0,2,1:T(8,128)}, u32[]{:S(2)}) copy-start(f32[256,8,128]{0,2,1:T(8,128)} %copy.180) | copy-start | bytes 3145732
  338.6 97.5 %copy-start.1 = (bf16[1024,1024]{1,0:T(8,128)(2,1)S(1)}, bf16[1024,1024]{1,0:T(8,128)(2,1)}, u32[]{:S(2)}) copy-start(bf16[1024,1024]{1,0:T(8,128)(2,1)} %param.18) | copy-start | bytes 6291460
Sparse Core Ops, SparseCore 0:
  338.6 94.6 all-reduce.1
where the time goes:
time: 451 us; the launch traced here: 443 us
  waiting for transfers between devices  171 us (38%)
  blocking collectives  79.4 us (18%)
  other arithmetic  57.6 us (13%)
  local copies, waits for them, and re-layouts  49.2 us (11%)
  matrix products  41.7 us (9%)
  starting transfers between devices  29 us (6%)
  between operations  14.8 us (3%)
    psum x1, waiting for transfers between devices, local(): lax.psum(table_part.astype(jnp.bfloat16), 'grp').astype(jnp.float32)  88.3 us
    ppermute x6, waiting for transfers between devices, from_behind(): lax.ppermute(value, axis, [(source, source + steps) for source in range(i...  83.2 us
    all_to_all x1, blocking collectives, local(): lax.all_to_all(jnp.concatenate([neg_grads, pos_grads], 1).astype(jnp.bflo...  54.9 us
    all_to_all x1, blocking collectives, fetch_items(): lax.all_to_all(wanted, 'seq', split_axis=0, concat_axis=0, tiled=True)  24.5 us
    ppermute x6, starting transfers between devices, from_behind(): lax.ppermute(value, axis, [(source, source + steps) for source in range(i...  21.5 us
    dot_general x3, matrix products, block_loss(): jnp.einsum('ipd,xpd->pix', query_unit, neg_unit, precision=highest)  16.9 us
    scatter-add x1, other arithmetic, local(): table_part = jnp.zeros((item_table.shape[0], model_width), jnp.float32).a...  14.5 us
  transfers between devices with their start and end apart: 8, of which 4 were waited for; matrix products, arithmetic and copies ran while one was open for 8% of the time, Pallas kernels for 0%

commit v1 on v0

v1 whole, which is shorter than its diff:
```python
import math

import jax
import jax.numpy as jnp
from jax import lax
from jax.experimental import pallas as pl
from jax.experimental.pallas import tpu as pltpu
from jax.sharding import Mesh
from jax.sharding import PartitionSpec as P

HEADS = 4
PARTS_SIZE = 8
INV_TEMP = 32.0
GATE_SCALE = 2.0

D = 1024
TOK = 256
NEG = 512
ITEMS = 512
CAPN = 16
CAPP = 8
CAP = CAPN + CAPP
PEERS = 32
HALF_ROWS = PEERS * CAP
QUARTER = ITEMS // 4
QKW = 256
PW = D // PARTS_SIZE
TILE = 16

PLANE = ("y", "x", "core")
SEQ = ("y", "zh", "x", "core")
COLUMN = ("zh", "grp")

F32 = jnp.float32
BF16 = jnp.bfloat16
HIGHEST = lax.Precision.HIGHEST


def matmul(a, b):
    return jnp.dot(a, b, preferred_element_type=F32)


def matmul_nt(a, b, precision=None):
    return lax.dot_general(a, b, (((1,), (1,)), ((), ())), precision=precision, preferred_element_type=F32)


def matmul_tn(a, b, precision=None):
    return lax.dot_general(a, b, (((0,), (0,)), ((), ())), precision=precision, preferred_element_type=F32)


def vmem_call(body, outs, n_smem=0, n_any=0, scratch=(), limit=50, flops=0, moved=0, name=None):
    def call(*args):
        in_specs = [pl.BlockSpec(memory_space=pltpu.SMEM)] * n_smem
        in_specs += [pl.BlockSpec(memory_space=pl.ANY)] * n_any
        in_specs += [pl.BlockSpec(memory_space=pltpu.VMEM)] * (len(args) - n_smem - n_any)
        return pl.pallas_call(
            body,
            out_shape=outs,
            in_specs=in_specs,
            out_specs=jax.tree.map(lambda _: pl.BlockSpec(memory_space=pltpu.VMEM), outs),
            scratch_shapes=list(scratch),
            compiler_params=pltpu.CompilerParams(vmem_limit_bytes=limit * 2**20),
            cost_estimate=pl.CostEstimate(flops=flops, bytes_accessed=moved, transcendentals=0),
            name=name,
        )(*args)

    return call


def pack_body(half_ref, nown_ref, nslot_ref, pown_ref, pslot_ref, ask_ref, place_ref, back_ref, owner_ref, slot_ref, sems):
    total = NEG + TOK
    pairs = (
        (nown_ref, owner_ref.at[:, :NEG]),
        (nslot_ref, slot_ref.at[:, :NEG]),
        (pown_ref, owner_ref.at[:, NEG:]),
        (pslot_ref, slot_ref.at[:, NEG:]),
    )
    copies = [pltpu.make_async_copy(a, b, sems.at[i]) for i, (a, b) in enumerate(pairs)]
    for copy in copies:
        copy.start()
    for copy in copies:
        copy.wait()
    owner = owner_ref[...]
    slot = slot_ref[...]
    lane = lax.broadcasted_iota(jnp.int32, (1, total), 1)
    positive = (lane >= NEG).astype(jnp.int32)
    far = ((owner >> 3) & 1) ^ half_ref[0]
    peer = (owner >> 4) * 8 + (owner & 7)
    key = positive * 64 + far * 32 + peer
    hot = key == lax.broadcasted_iota(jnp.int32, (128, total), 0)
    before = lax.broadcasted_iota(jnp.int32, (total, total), 0) < lax.broadcasted_iota(jnp.int32, (total, total), 1)
    counts = matmul(hot.astype(F32).astype(BF16), before.astype(F32).astype(BF16))
    rank = jnp.sum(jnp.where(hot, counts, 0.0), 0, keepdims=True).astype(jnp.int32)
    inner = rank + positive * CAPN
    column = far * CAP + inner
    peer_hot = (peer == lax.broadcasted_iota(jnp.int32, (PEERS, total), 0)).astype(F32).astype(BF16)
    here = column == lax.broadcasted_iota(jnp.int32, (2 * CAP, total), 0)
    value = slot + 1
    high = jnp.where(here, (value >> 5).astype(F32), 0.0).astype(BF16)
    low = jnp.where(here, (value & 31).astype(F32), 0.0).astype(BF16)
    ids = matmul_nt(peer_hot, high) * 32.0 + matmul_nt(peer_hot, low)
    ask_ref[...] = ids.astype(jnp.int32) - 1
    place_ref[...] = far * HALF_ROWS + peer * CAP + inner
    back_ref[...] = peer * (2 * CAP) + column


def pack(half, neg_owner, neg_slot, pos_owner, pos_slot):
    outs = (
        jax.ShapeDtypeStruct((PEERS, 2 * CAP), jnp.int32),
        jax.ShapeDtypeStruct((1, NEG + TOK), jnp.int32),
        jax.ShapeDtypeStruct((1, NEG + TOK), jnp.int32),
    )
    row = pltpu.VMEM((1, NEG + TOK), jnp.int32)
    return vmem_call(
        pack_body, outs, n_smem=1, n_any=4, scratch=[row, row, pltpu.SemaphoreType.DMA((4,))], name="pack"
    )(half, neg_owner, neg_slot, pos_owner, pos_slot)


def look_body(ids_ref, table_ref, rows_ref):
    hot = ids_ref[...] == lax.broadcasted_iota(jnp.int32, (HALF_ROWS, ITEMS), 1)
    rows_ref[...] = matmul(hot.astype(F32).astype(BF16), table_ref[...]).astype(BF16)


def look(ids, table):
    outs = jax.ShapeDtypeStruct((HALF_ROWS, D), BF16)
    return vmem_call(look_body, outs, flops=2 * HALF_ROWS * ITEMS * D, moved=4 * 2**20, name="look")(ids, table)


def relay(own):
    ups, downs = [], []
    up = down = own
    for hop in range(3):
        up = lax.ppermute(up, "grp", [(i, i + 1) for i in range(hop, 3)])
        down = lax.ppermute(down, "grp", [(i + 1, i) for i in range(3 - hop)])
        ups.append(up)
        downs.append(down)
    return [own] + ups + downs


def lay_out(grp, own_ref, up_refs, down_refs, out_ref):
    def put(at, ref):
        out_ref[pl.ds(pl.multiple_of(at * QUARTER, QUARTER), QUARTER), :] = ref[...].astype(out_ref.dtype)

    put(grp, own_ref)
    for k in range(3):
        pl.when(grp > k)(lambda k=k: put(grp - k - 1, up_refs[k]))
        pl.when(grp < 3 - k)(lambda k=k: put(grp + k + 1, down_refs[k]))


def look_far_body(grp_ref, ids_ref, own_ref, u1, u2, u3, d1, d2, d3, rows_ref, table_ref):
    lay_out(grp_ref[0], own_ref, (u1, u2, u3), (d1, d2, d3), table_ref)
    look_body(ids_ref, table_ref, rows_ref)


def look_far(grp, ids, quarters):
    outs = jax.ShapeDtypeStruct((HALF_ROWS, D), BF16)
    return vmem_call(
        look_far_body, outs, n_smem=1, scratch=[pltpu.VMEM((ITEMS, D), BF16)], flops=2 * HALF_ROWS * ITEMS * D,
        moved=4 * 2**20, name="look_far",
    )(grp, ids, *quarters)


def spread_body(grp_ref, own_ref, u1, u2, u3, d1, d2, d3, out_ref):
    lay_out(grp_ref[0], own_ref, (u1, u2, u3), (d1, d2, d3), out_ref)


def spread(grp, quarters):
    outs = jax.ShapeDtypeStruct((ITEMS, D), F32)
    return vmem_call(spread_body, outs, n_smem=1, moved=3 * 2**20, name="spread")(grp, *quarters)


def add_body(ids_ref, grads_ref, table_ref):
    for part in range(4):
        size = 2 * ITEMS // 4
        row = lax.broadcasted_iota(jnp.int32, (size, 2 * HALF_ROWS), 0) + part * size
        hot = (ids_ref[...] == row).astype(F32).astype(BF16)
        table_ref[part * size : (part + 1) * size, :] = matmul(hot, grads_ref[...]).astype(BF16)


def add_up(ids, grads):
    outs = jax.ShapeDtypeStruct((2 * ITEMS, D), BF16)
    return vmem_call(add_body, outs, flops=8 * HALF_ROWS * ITEMS * D, moved=5 * 2**20, name="add_up")(ids, grads)


def layer_norm(values, gain_vec):
    average = jnp.mean(values, -1, keepdims=True)
    centred = values - average
    spread = jnp.mean(centred * centred, -1, keepdims=True)
    return centred * lax.rsqrt(spread + 1e-05) * gain_vec


def front_body(tok_ref, gain_ref, w_ref, gq_ref, kv_ref):
    normed = layer_norm(tok_ref[...].astype(F32), gain_ref[...]).astype(BF16)

    def project(first, size):
        half = 0.5 * matmul(normed, w_ref[:, first : first + size])
        return (half + half * jnp.tanh(half)).astype(BF16)

    for at in range(0, D, 512):
        kv_ref[:, at : at + 512] = project(D + at, 512)
    kv_ref[:, D:] = project(2 * D + QKW, QKW)
    for at in range(0, D, 512):
        gq_ref[:, at : at + 512] = project(at, 512)
    gq_ref[:, D:] = project(2 * D, QKW)


def front_kernel(own_tokens, in_gain, w_in):
    out = jax.ShapeDtypeStruct((TOK, D + QKW), BF16)
    return vmem_call(front_body, (out, out), flops=14 * 10**8, moved=7 * 2**20, name="front")(own_tokens, in_gain, w_in)


def attend_body(grp_ref, len_ref, tok_ref, gq_ref, kv0_ref, kv1_ref, kv2_ref, kv3_ref, gain_ref, wout_ref, out_ref, mixed_ref):
    start = grp_ref[0] * TOK
    ends = [len_ref[0, 0]]
    for i in range(1, len_ref.shape[1]):
        ends.append(ends[-1] + len_ref[0, i])

    def segment(pos):
        return sum((pos >= end).astype(jnp.int32) for end in ends)

    query_pos = start + lax.broadcasted_iota(jnp.int32, (TOK, 1), 0)
    query_seg = segment(query_pos)
    masks = []
    for hop in range(4):
        key_pos = start - hop * TOK + lax.broadcasted_iota(jnp.int32, (1, TOK), 1)
        seen = (query_seg == segment(key_pos)) & (key_pos >= 0) & (key_pos <= query_pos)
        masks.append(jnp.where(seen, 0.5 / math.sqrt(QKW // HEADS), 0.0))
    qkh = QKW // HEADS
    vh = D // HEADS
    for head in range(HEADS):
        query = gq_ref[:, D + head * qkh : D + (head + 1) * qkh]
        acc = jnp.zeros((TOK, vh), F32)
        for hop, ref in enumerate((kv0_ref, kv1_ref, kv2_ref, kv3_ref)):
            key = ref[:, D + head * qkh : D + (head + 1) * qkh]
            value = ref[:, head * vh : (head + 1) * vh]
            scores = matmul_nt(query, key) * masks[hop]
            weights = (scores + scores * jnp.tanh(scores)).astype(BF16)
            acc = acc + matmul(weights, value)
        mixed_ref[:, head * vh : (head + 1) * vh] = acc
    gated = (layer_norm(mixed_ref[...], gain_ref[...]) * gq_ref[:, :D].astype(F32)).astype(BF16)
    out_ref[...] = tok_ref[...].astype(F32) + matmul(gated, wout_ref[...])


def attend(grp, lengths, own_tokens, gq, kvs, out_gain, w_out):
    outs = jax.ShapeDtypeStruct((TOK, D), F32)
    return vmem_call(
        attend_body, outs, n_smem=2, scratch=[pltpu.VMEM((TOK, D), F32)], flops=2 * 10**9, moved=8 * 2**20, name="attend"
    )(grp, lengths, own_tokens, gq, *kvs, out_gain, w_out)


def gate_of(u):
    t = jnp.tanh(u)
    return t, jnp.exp(GATE_SCALE * t)


def split(values):
    high = values.astype(BF16).astype(F32)
    return high, values - high


def split_rows(values):
    high, rest = split(values)
    middle, low = split(rest)
    return jnp.concatenate([high, middle, low], 0).astype(BF16)


def loss_body(
    query_ref, near_ref, far_ref, place_ref, back_ref, wqt_ref, wxt_ref,
    loss_ref, qgrad_ref, grads_ref,
    x_ref, unit_ref, cos_ref, dcos_ref, dcosr_ref, side_ref, dqgate_ref, dxgate_ref, dx_ref, du_ref,
):
    lanes = lax.broadcasted_iota(jnp.int32, (NEG + TOK, HALF_ROWS), 1)
    hot_near = (place_ref[...] == lanes).astype(F32).astype(BF16)
    hot_far = (place_ref[...] == lanes + HALF_ROWS).astype(F32).astype(BF16)
    x_ref[...] = (matmul(hot_near, near_ref[...]) + matmul(hot_far, far_ref[...])).astype(BF16)

    part_of = lax.broadcasted_iota(jnp.int32, (16, D), 1) // PW
    pick = (part_of == lax.broadcasted_iota(jnp.int32, (16, D), 0)).astype(F32).astype(BF16)
    eye = lax.broadcasted_iota(jnp.int32, (1, PARTS_SIZE), 1)

    rows = x_ref[...].astype(F32)
    high, low = split(rows * rows)
    squares = matmul_nt(high.astype(BF16), pick) + matmul_nt(low.astype(BF16), pick)
    x_norms = lax.rsqrt(squares[:, :PARTS_SIZE] + 1e-06)
    terms = matmul_nt(x_ref[...], split_rows(wxt_ref[...]))
    xgate = terms[:, :8] + terms[:, 8:16] + terms[:, 16:]
    side = jnp.concatenate([xgate[:NEG], x_norms[:NEG], jnp.zeros((NEG, 112), F32)], 1)
    side_ref[...] = jnp.transpose(side)[:16, :]
    pgate = xgate[NEG:]

    query = query_ref[...]
    qgate = matmul_nt(query, wqt_ref[...], HIGHEST)

    pos_cos = jnp.zeros((TOK, PARTS_SIZE), F32)
    q_norms = []
    for p in range(PARTS_SIZE):
        cols = slice(p * PW, (p + 1) * PW)
        q_p = query_ref[:, cols]
        q_norm = lax.rsqrt(jnp.sum(q_p * q_p, -1, keepdims=True) + 1e-06)
        q_unit = q_p * q_norm
        unit_ref[:, cols] = q_unit
        q_high, q_low = split(q_unit)
        x_p = x_ref[:NEG, cols]
        q_two = jnp.concatenate([q_high.astype(BF16), q_low.astype(BF16)], 1)
        cos_ref[p] = matmul_nt(q_two, jnp.concatenate([x_p, x_p], 1)) * side_ref[8 + p : 9 + p, :]
        dot_p = jnp.sum(q_unit * x_ref[NEG:, cols].astype(F32), -1, keepdims=True)
        pos_cos = jnp.where(eye == p, dot_p, pos_cos)
        q_norms.append(q_norm)
    pos_cos = pos_cos * x_norms[NEG:]

    t_pos, e_pos = gate_of(qgate + pgate)
    mix_pos = e_pos / jnp.sum(e_pos, -1, keepdims=True)
    mean_pos = jnp.sum(mix_pos * pos_cos, -1, keepdims=True)
    pos_logit = INV_TEMP * mean_pos
    raised_pos = jnp.exp(pos_logit)

    dxgate_ref[...] = jnp.zeros_like(dxgate_ref)
    dqgate_ref[...] = qgate
    loss_ref[...] = raised_pos

    def tile(i, carry):
        rows = pl.ds(pl.multiple_of(i * TILE, TILE), TILE)
        qg = dqgate_ref[rows, :]
        qgs = [jnp.broadcast_to(qg[:, p : p + 1], (TILE, PW)) for p in range(PARTS_SIZE)]
        sums = [jnp.zeros((TILE, PW), F32) for _ in range(PARTS_SIZE)]
        part = jnp.zeros((TILE, PW), F32)
        for block in range(NEG // PW):
            cols = slice(block * PW, (block + 1) * PW)
            ts, es, cs = [], [], []
            total = jnp.zeros((TILE, PW), F32)
            mixed = jnp.zeros((TILE, PW), F32)
            for p in range(PARTS_SIZE):
                t, e = gate_of(qgs[p] + side_ref[p : p + 1, cols])
                c = cos_ref[p, rows, cols]
                total = total + e
                mixed = mixed + e * c
                ts.append(t)
                es.append(e)
                cs.append(c)
            inverse = 1.0 / total
            mean = mixed * inverse
            raised = jnp.exp(INV_TEMP * mean)
            part = part + raised
            scaled = raised * inverse
            for p in range(PARTS_SIZE):
                dcos = scaled * es[p]
                du = dcos * (cs[p] - mean) * (1.0 - ts[p] * ts[p])
                dcos_ref[p, rows, cols] = dcos.astype(BF16)
                dcosr_ref[p, rows, cols] = (dcos * side_ref[8 + p : 9 + p, cols]).astype(BF16)
                du_ref[p, :, cols] = du
                sums[p] = sums[p] + du
        partition = loss_ref[rows, :] + jnp.sum(part, -1, keepdims=True)
        factor = (GATE_SCALE * INV_TEMP) / partition
        dq = jnp.zeros((TILE, PARTS_SIZE), F32)
        for p in range(PARTS_SIZE):
            du = du_ref[p] * factor
            dxgate_ref[p] += du[:8] + du[8:]
            dq = jnp.where(eye == p, jnp.sum(sums[p], -1, keepdims=True), dq)
        dqgate_ref[rows, :] = dq * factor
        loss_ref[rows, :] = partition
        return carry

    lax.fori_loop(0, TOK // TILE, tile, 0, unroll=2)

    partition = loss_ref[...]
    loss_ref[...] = jnp.log(partition) - pos_logit
    share = INV_TEMP / partition
    dpos = INV_TEMP * (raised_pos / partition - 1.0)
    dcos_pos = dpos * mix_pos
    du_pos = dcos_pos * (pos_cos - mean_pos) * (GATE_SCALE - GATE_SCALE * t_pos * t_pos)
    dxgate = jnp.transpose(jnp.concatenate([jnp.sum(dxgate_ref[...], 1), jnp.zeros((120, NEG), F32)], 0))

    def by_gate(values):
        high, low = split(values)
        return jnp.concatenate([high, low, high], 1).astype(BF16)

    def gate_weights(values):
        high, low = split(values)
        return jnp.concatenate([high, high, low], 0).astype(BF16)

    dqgate = by_gate(dqgate_ref[...] + du_pos)
    dxgate = by_gate(jnp.concatenate([dxgate[:, :PARTS_SIZE], du_pos], 0))
    wq = gate_weights(wqt_ref[...])
    wx = gate_weights(wxt_ref[...])

    for p in range(PARTS_SIZE):
        cols = slice(p * PW, (p + 1) * PW)
        q_unit = unit_ref[:, cols]
        dc = dcos_pos[:, p : p + 1]
        p_norm = x_norms[NEG:, p : p + 1]
        p_unit = x_ref[NEG:, cols].astype(F32) * p_norm
        d_unit = matmul(dcosr_ref[p], x_ref[:NEG, cols]) * share + dc * p_unit
        along = jnp.sum(d_unit * q_unit, -1, keepdims=True)
        qgrad_ref[:, cols] = (q_norms[p] * (d_unit - q_unit * along) + matmul(dqgate, wq[:, cols])).astype(BF16)

        gate_term = matmul(dxgate, wx[:, cols])
        dpos_p = p_norm * dc * (q_unit - p_unit * pos_cos[:, p : p + 1]) + gate_term[NEG:]
        dx_ref[NEG:, cols] = dpos_p.astype(BF16)

        x_norm = x_norms[:NEG, p : p + 1]
        x_unit = x_ref[:NEG, cols].astype(F32) * x_norm
        d_unit = matmul_tn(dcos_ref[p], (q_unit * share).astype(BF16))
        along = jnp.sum(d_unit * x_unit, -1, keepdims=True)
        dx_ref[:NEG, cols] = (x_norm * (d_unit - x_unit * along) + gate_term[:NEG]).astype(BF16)

    for part in range(4):
        size = 2 * HALF_ROWS // 4
        row = lax.broadcasted_iota(jnp.int32, (size, NEG + TOK), 0) + part * size
        hot = (back_ref[...] == row).astype(F32).astype(BF16)
        grads_ref[part * size : (part + 1) * size, :] = matmul(hot, dx_ref[...]).astype(BF16)


def loss_and_grads(query, near, far, place, back, w_qgate, w_xgate):
    outs = (
        jax.ShapeDtypeStruct((TOK, 1), F32),
        jax.ShapeDtypeStruct((TOK, D), BF16),
        jax.ShapeDtypeStruct((2 * HALF_ROWS, D), BF16),
    )
    scratch = [
        pltpu.VMEM((NEG + TOK, D), BF16),
        pltpu.VMEM((TOK, D), F32),
        pltpu.VMEM((PARTS_SIZE, TOK, NEG), F32),
        pltpu.VMEM((PARTS_SIZE, TOK, NEG), BF16),
        pltpu.VMEM((PARTS_SIZE, TOK, NEG), BF16),
        pltpu.VMEM((2 * PARTS_SIZE, NEG), F32),
        pltpu.VMEM((TOK, PARTS_SIZE), F32),
        pltpu.VMEM((PARTS_SIZE, 8, NEG), F32),
        pltpu.VMEM((NEG + TOK, D), BF16),
        pltpu.VMEM((PARTS_SIZE, TILE, NEG), F32),
    ]
    return vmem_call(loss_body, outs, scratch=scratch, flops=8 * 10**9, moved=10 * 2**20, name="loss")(
        query, near, far, place.reshape(-1, 1), back, w_qgate.T, w_xgate.T
    )


def local(
    tokens,
    lengths,
    in_gain,
    out_gain,
    w_in,
    w_out,
    w_qgate,
    w_xgate,
    item_table,
    neg_owner,
    neg_slot,
    pos_owner,
    pos_slot,
):
    own_tokens = tokens[0]
    half = lax.axis_index("zh").astype(jnp.int32)[None]
    grp = lax.axis_index("grp").astype(jnp.int32)[None]
    barrier = lax.optimization_barrier

    moved = lax.dynamic_slice_in_dim(item_table, grp[0] * QUARTER, QUARTER, 0)
    half_then, _ = barrier((half, moved))
    moved = lax.ppermute(moved, "zh", [(0, 1), (1, 0)])

    ask, place, back = pack(
        half_then,
        neg_owner.reshape(1, NEG),
        neg_slot.reshape(1, NEG),
        pos_owner.reshape(1, TOK),
        pos_slot.reshape(1, TOK),
    )
    asked = lax.all_to_all(ask, PLANE, split_axis=0, concat_axis=0, tiled=True)

    gate_query, key_value = front_kernel(own_tokens, in_gain[None], w_in)
    kvs = [key_value]
    for hop in range(3):
        kvs.append(lax.ppermute(kvs[-1], "grp", [(i, i + 1) for i in range(3)]))
    quarters = relay(moved)

    asked_then, _, _ = barrier((asked, key_value, moved))
    near_ids = asked_then[:, :CAP].reshape(-1, 1)
    far_ids = asked_then[:, CAP:].reshape(-1, 1)
    near = lax.all_to_all(look(near_ids, item_table), PLANE, split_axis=0, concat_axis=0, tiled=True)
    far_ids, _ = barrier((far_ids, kvs[2]))
    far = lax.all_to_all(look_far(grp, far_ids, quarters), PLANE, split_axis=0, concat_axis=0, tiled=True)

    query = attend(grp, lengths, own_tokens, gate_query, kvs, out_gain[None], w_out)

    losses, query_grad, grads = loss_and_grads(query, near, far, place, back, w_qgate, w_xgate)

    came = lax.all_to_all(grads, PLANE, split_axis=0, concat_axis=0, tiled=True)
    shard = half[0] ^ (lax.broadcasted_iota(jnp.int32, asked.shape, 1) // CAP)
    rows = jnp.where(asked >= 0, asked + shard * ITEMS, -1).reshape(1, -1)
    table = add_up(rows, came)
    table = lax.psum_scatter(table, COLUMN, tiled=True)
    return (losses.reshape(1, TOK), query_grad[None], spread(grp, relay(table)))


def solution(mesh):
    fine = Mesh(mesh.devices.reshape(4, 4, 2, 4, 2), ("grp", "y", "zh", "x", "core"))
    in_specs = (
        P(SEQ, "grp", None),
        P(SEQ, None),
        P(),
        P(),
        P(),
        P(),
        P(),
        P(),
        P(SEQ, None),
        P(SEQ, "grp", None),
        P(SEQ, "grp"),
        P(SEQ, "grp", None),
        P(SEQ, "grp"),
    )
    out_specs = (P(SEQ, "grp"), P(SEQ, "grp", None), P(SEQ, None))
    return jax.shard_map(local, mesh=fine, in_specs=in_specs, out_specs=out_specs, check_vma=False)
```

time: 451 us -> 287 us (0.64); the launches traced: 443 us -> 286 us
  blocking collectives: 79.4 us -> 0 us
  other arithmetic: 57.6 us -> 1.4 us
  starting transfers between devices: 29 us -> 74.8 us
  Pallas kernels: 0 us -> 44.5 us
  matrix products: 41.7 us -> 0 us
  local copies, waits for them, and re-layouts: 49.2 us -> 12.6 us
  waiting for transfers between devices: 171 us -> 138 us
    psum x1 -> x0, waiting for transfers between devices: 88.3 us -> none  [local(): lax.psum(table_part.astype(jnp.bfloat16), 'grp').astype(jnp.float32)]
    all_to_all x2 -> x0, blocking collectives: 79.4 us -> none  [the longest x1 54.9 us: local(): lax.all_to_all(jnp.concatenate([neg_grads, pos_grads], 1).astype(jnp.bflo...]
    reduce_scatter x0 -> x1, waiting for transfers between devices: none -> 49.5 us  [local(): table = lax.psum_scatter(table, COLUMN, tiled=True)]
    pallas_call x0 -> x8, Pallas kernels: none -> 44.5 us  [call(): pl.pallas_call(body, out_shape=outs, in_specs=in_specs, out_specs=jax.tre...]
    dot_general x12 -> x0, matrix products: 41.7 us -> none  [the longest x3 16.9 us: block_loss(): jnp.einsum('ipd,xpd->pix', query_unit, neg_unit, precision=highest)]
    all_to_all x1 -> x4, waiting for transfers between devices: 0.01 us -> 36.3 us  [the longest x1 36.3 us: local(): came = lax.all_to_all(grads, PLANE, split_axis=0, concat_axis=0, tiled=True)]
    ppermute x6 -> x16, waiting for transfers between devices: 83.2 us -> 52.2 us  [the longest x6 27.7 us: relay(): down = lax.ppermute(down, 'grp', [(i + 1, i) for i in range(3 - hop)])]
    ppermute x6 -> x16, starting transfers between devices: 21.5 us -> 44.7 us  [the longest x3 17.1 us: local(): kvs.append(lax.ppermute(kvs[-1], 'grp', [(i, i + 1) for i in range(3)]))]
  transfers between devices with their start and end apart: 8 -> 21, of which waited for: 4 -> 10; matrix products, arithmetic and copies ran while one was open for 8% -> 1% of each run, Pallas kernels for 0% -> 5%
where the time goes in v1:
time: 287 us; the launch traced here: 286 us
  waiting for transfers between devices  138 us (48%)
  starting transfers between devices  74.8 us (26%)
  Pallas kernels  44.5 us (16%)
  between operations  14.4 us (5%)
  local copies, waits for them, and re-layouts  12.6 us (4%)
    reduce_scatter x1, waiting for transfers between devices, local(): table = lax.psum_scatter(table, COLUMN, tiled=True)  49.5 us
    pallas_call x8, Pallas kernels, call(): pl.pallas_call(body, out_shape=outs, in_specs=in_specs, out_specs=jax.tre...  44.5 us
    all_to_all x1, waiting for transfers between devices, local(): came = lax.all_to_all(grads, PLANE, split_axis=0, concat_axis=0, tiled=True)  36.3 us
    ppermute x6, waiting for transfers between devices, relay(): down = lax.ppermute(down, 'grp', [(i + 1, i) for i in range(3 - hop)])  27.7 us
    ppermute x3, waiting for transfers between devices, local(): kvs.append(lax.ppermute(kvs[-1], 'grp', [(i, i + 1) for i in range(3)]))  24.4 us
    ppermute x3, starting transfers between devices, local(): kvs.append(lax.ppermute(kvs[-1], 'grp', [(i, i + 1) for i in range(3)]))  17.1 us
    ppermute x6, starting transfers between devices, relay(): up = lax.ppermute(up, 'grp', [(i, i + 1) for i in range(hop, 3)])  12.5 us
    unnamed x42, local copies, waits for them, and re-layouts  10.2 us
  transfers between devices with their start and end apart: 21, of which 10 were waited for; matrix products, arithmetic and copies ran while one was open for 1% of the time, Pallas kernels for 5%

profile of v1, /device:TPU:4, one launch (start us, length us, event | category | flops | bytes accessed | tf_op | source)
XLA Modules:
  0.0 285.6 jit_solution(3807157226945967809)
XLA Ops:
  8.1 7.3 %collective-permute-start.3 = (bf16[128,1024]{1,0:T(8,128)(2,1)S(1)}, bf16[128,1024]{1,0:T(8,128)(2,1)S(1)}, u32[]{:S(2)}, u32[]{:S(2)}) collective-permute-start(bf16[128,1024]{1,0:T(8,128)(2,1)S(1)} %constant_dynamic-slice_fusion), channel_id=1, source_target_pairs={{0,8},{8,0},{1,9},{9,1},{2,10},{10,2},{3,11},{11,3},{4,12},{12,4},... | collective-permute-start | bytes 786440 | tf_op jit(solution)/shard_map/ppermute | solution.py:458
  19.4 7.6 %all-to-all-start = ((s32[32,1,48]{2,1,0:T(1,128)}), s32[32,1,48]{2,1,0:T(1,128)S(1)}, u32[]{:S(2)}, u32[]{:S(2)}) async-start(s32[32,1,48]{2,1,0:T(1,128)} %bitcast.8), calls=%async_computation | async-start | bytes 32768 | tf_op jit(solution)/shard_map/all_to_all | solution.py:467
  28.7 4.5 %front.1 = (bf16[256,1280]{1,0:T(8,128)(2,1)S(1)}, bf16[256,1280]{1,0:T(8,128)(2,1)S(1)}) custom-call(bf16[256,1024]{1,0:T(8,128)(2,1)S(1)} %bitcast.23, f32[1,1024]{1,0:T(1,128)S(1)} %bitcast.25, bf16[1024,2560]{1,0:T(8,128)(2,1)} %w_ref.1), custom_call_target="tpu_custom_call" | custom-call | flops 1400000000 | bytes 7340032 | tf_op jit(solution)/shard_map/front/pallas_call | solution.py:56
  34.3 2.2 look.1
  36.5 7.4 %all-to-all-start.1 = ((bf16[32,24,1024]{2,1,0:T(8,128)(2,1)}), bf16[32,24,1024]{2,1,0:T(8,128)(2,1)S(1)}, u32[]{:S(2)}, u32[]{:S(2)}) async-start(bf16[32,24,1024]{2,1,0:T(8,128)(2,1)} %bitcast.10), calls=%async_computation.1 | async-start | bytes 3145728 | tf_op jit(solution)/shard_map/all_to_all | solution.py:478
  43.9 3.8 %collective-permute-start = (bf16[256,1280]{1,0:T(8,128)(2,1)S(1)}, bf16[256,1280]{1,0:T(8,128)(2,1)}, u32[]{:S(2)}, u32[]{:S(2)}) collective-permute-start(bf16[256,1280]{1,0:T(8,128)(2,1)S(1)} %get-tuple-element.15.kv0_ref), channel_id=1, source_target_pairs={{0,64},{64,128},{128,192},{1,65},{65,129},{129,193},{2,66},{66,130... | collective-permute-start | bytes 1966088 | tf_op jit(solution)/shard_map/ppermute | solution.py:472
  49.0 4.6 %collective-permute-start.4 = (bf16[128,1024]{1,0:T(8,128)(2,1)S(1)}, bf16[128,1024]{1,0:T(8,128)(2,1)S(1)}, u32[]{:S(2)}, u32[]{:S(2)}) collective-permute-start(bf16[128,1024]{1,0:T(8,128)(2,1)S(1)} %collective-permute-done.3.own_ref), channel_id=1, source_target_pairs={{0,64},{64,128},{128,192},{1,65},{65,129},{129,193},{2,66},{66,130... | collective-permute-start | bytes 786440 | tf_op jit(solution)/shard_map/ppermute | solution.py:133
  53.5 8.4 %collective-permute-done.kv1_ref = bf16[256,1280]{1,0:T(8,128)(2,1)} collective-permute-done((bf16[256,1280]{1,0:T(8,128)(2,1)S(1)}, bf16[256,1280]{1,0:T(8,128)(2,1)}, u32[]{:S(2)}, u32[]{:S(2)}) %collective-permute-start) | collective-permute-done | bytes 655392 | tf_op jit(solution)/shard_map/ppermute | solution.py:472
  61.9 5.3 %collective-permute-start.1 = (bf16[256,1280]{1,0:T(8,128)(2,1)}, bf16[256,1280]{1,0:T(8,128)(2,1)}, u32[]{:S(2)}, u32[]{:S(2)}) collective-permute-start(bf16[256,1280]{1,0:T(8,128)(2,1)} %collective-permute-done.kv1_ref), channel_id=1, source_target_pairs={{0,64},{64,128},{128,192},{1,65},{65,129},{129,193},{2,66},{66,130... | collective-permute-start | bytes 1966088 | tf_op jit(solution)/shard_map/ppermute | solution.py:472
  67.2 1.3 collective-permute-start.8
  69.2 6.4 %collective-permute-done.8.d2 = bf16[128,1024]{1,0:T(8,128)(2,1)S(1)} collective-permute-done((bf16[128,1024]{1,0:T(8,128)(2,1)S(1)}, bf16[128,1024]{1,0:T(8,128)(2,1)S(1)}, u32[]{:S(2)}, u32[]{:S(2)}) %collective-permute-start.8) | collective-permute-done | bytes 262176 | tf_op jit(solution)/shard_map/ppermute | solution.py:134
  75.6 1.3 collective-permute-start.9
  76.9 1.4 collective-permute-start.6
  78.4 2.5 collective-permute-done.1.kv2_ref
  81.1 2.8 collective-permute-done.9.d3
  83.8 3.2 %look_far.1 = bf16[768,1024]{1,0:T(8,128)(2,1)} custom-call(s32[1]{0:T(128)} %bitcast.grp_ref, s32[768,1]{1,0:T(8,128)S(1)} %copy.21.ids_ref, bf16[128,1024]{1,0:T(8,128)(2,1)S(1)} %collective-permute-done.3.own_ref, bf16[128,1024]{1,0:T(8,128)(2,1)S(1)} %collective-permute-done.4.u1, bf16[128,1024]{1,0:T(8,128)(2,1)S(1)} %collective-permute-done.5.u2, ...), custom_call_target="tpu_custom_call" | custom-call | flops 805306368 | bytes 4194304 | tf_op jit(solution)/shard_map/look_far/pallas_call | solution.py:56
  87.1 7.6 %all-to-all-start.2 = ((bf16[32,24,1024]{2,1,0:T(8,128)(2,1)}), bf16[32,24,1024]{2,1,0:T(8,128)(2,1)}, u32[]{:S(2)}, u32[]{:S(2)}) async-start(bf16[32,24,1024]{2,1,0:T(8,128)(2,1)} %bitcast.12), calls=%async_computation.2 | async-start | bytes 3145728 | tf_op jit(solution)/shard_map/all_to_all | solution.py:480
  94.7 8.0 %collective-permute-start.2 = (bf16[256,1280]{1,0:T(8,128)(2,1)}, bf16[256,1280]{1,0:T(8,128)(2,1)}, u32[]{:S(2)}, u32[]{:S(2)}) collective-permute-start(bf16[256,1280]{1,0:T(8,128)(2,1)} %collective-permute-done.1.kv2_ref), channel_id=1, source_target_pairs={{0,64},{64,128},{128,192},{1,65},{65,129},{129,193},{2,66},{66,130... | collective-permute-start | bytes 1966088 | tf_op jit(solution)/shard_map/ppermute | solution.py:472
  102.9 13.6 %collective-permute-done.2.kv3_ref = bf16[256,1280]{1,0:T(8,128)(2,1)} collective-permute-done((bf16[256,1280]{1,0:T(8,128)(2,1)}, bf16[256,1280]{1,0:T(8,128)(2,1)}, u32[]{:S(2)}, u32[]{:S(2)}) %collective-permute-start.2) | collective-permute-done | bytes 655392 | tf_op jit(solution)/shard_map/ppermute | solution.py:472
  117.6 5.6 %attend.1.query_ref = f32[256,1024]{1,0:T(8,128)} custom-call(s32[1]{0:T(128)} %bitcast.grp_ref, s32[1,3]{1,0:T(1,128)S(1)} %copy-done.16, bf16[256,1024]{1,0:T(8,128)(2,1)S(1)} %bitcast.24, bf16[256,1280]{1,0:T(8,128)(2,1)S(1)} %copy-done.10, bf16[256,1280]{1,0:T(8,128)(2,1)S(1)} %copy-done.12, bf16[256,1280]{1,0:T(8,128)(2,1)} %collective-permute-done.kv1_ref, ...), custom_call_target="tpu_custom_call" | custom-call | flops 2000000000 | bytes 8388608 | tf_op jit(solution)/shard_map/attend/pallas_call | solution.py:56
  124.4 19.7 %loss.1 = (f32[256,1]{1,0:T(8,128)S(1)}, bf16[256,1024]{1,0:T(8,128)(2,1)}, bf16[1536,1024]{1,0:T(8,128)(2,1)}) custom-call(f32[256,1024]{1,0:T(8,128)S(1)} %copy-done.17, bf16[768,1024]{1,0:T(8,128)(2,1)S(1)} %bitcast.22, bf16[768,1024]{1,0:T(8,128)(2,1)} %bitcast.13.far_ref, s32[768,1]{1,0:T(8,128)S(1)} %copy.22.place_ref, ...), custom_call_target="tpu_custom_call" | custom-call | flops 8000000000 | bytes 10485760 | tf_op jit(solution)/shard_map/loss/pallas_call | solution.py:56
  144.1 7.5 %all-to-all-start.3 = ((bf16[32,48,1024]{2,1,0:T(8,128)(2,1)}), bf16[32,48,1024]{2,1,0:T(8,128)(2,1)S(1)}, u32[]{:S(2)}, u32[]{:S(2)}) async-start(bf16[32,48,1024]{2,1,0:T(8,128)(2,1)} %bitcast.32), calls=%async_computation.3 | async-start | bytes 6291456 | tf_op jit(solution)/shard_map/all_to_all | solution.py:486
  153.1 36.3 %all-to-all-done.3 = bf16[32,48,1024]{2,1,0:T(8,128)(2,1)S(1)} async-done(((bf16[32,48,1024]{2,1,0:T(8,128)(2,1)}), bf16[32,48,1024]{2,1,0:T(8,128)(2,1)S(1)}, u32[]{:S(2)}, u32[]{:S(2)}) %all-to-all-start.3) | async-done | bytes 3145760 | tf_op jit(solution)/shard_map/all_to_all | solution.py:486
  189.4 1.6 copy-done.18
  191.0 6.6 %add_up.1 = bf16[1024,1024]{1,0:T(8,128)(2,1)} custom-call(s32[1,1536]{1,0:T(1,128)S(1)} %compare_select_fusion.ids_ref, bf16[1536,1024]{1,0:T(8,128)(2,1)} %bitcast.33), custom_call_target="tpu_custom_call" | custom-call | flops 3221225472 | bytes 5242880 | tf_op jit(solution)/shard_map/add_up/pallas_call | solution.py:56
  197.7 49.5 %reduce-scatter.2.cloned.1.call-done.own_ref = bf16[128,1024]{1,0:T(8,128)(2,1)} async-done(((bf16[1024,1024]{1,0:T(8,128)(2,1)}), bf16[128,1024]{1,0:T(8,128)(2,1)}) %reduce-scatter.2.cloned.1.call-update) | async-done | bytes 262160 | tf_op jit(solution)/shard_map/reduce_scatter | solution.py:490
  248.5 4.6 %collective-permute-start.10 = (bf16[128,1024]{1,0:T(8,128)(2,1)}, bf16[128,1024]{1,0:T(8,128)(2,1)S(1)}, u32[]{:S(2)}, u32[]{:S(2)}) collective-permute-start(bf16[128,1024]{1,0:T(8,128)(2,1)} %reduce-scatter.2.cloned.1.call-done.own_ref), channel_id=1, source_target_pairs={{0,64},{64,128},{128,192},{1,65},{65,129},{129,193},{2,66},{66,130... | collective-permute-start | bytes 786440 | tf_op jit(solution)/shard_map/ppermute | solution.py:133
  253.0 4.1 %collective-permute-done.13.d1 = bf16[128,1024]{1,0:T(8,128)(2,1)S(1)} collective-permute-done((bf16[128,1024]{1,0:T(8,128)(2,1)}, bf16[128,1024]{1,0:T(8,128)(2,1)S(1)}, u32[]{:S(2)}, u32[]{:S(2)}) %collective-permute-start.13) | collective-permute-done | bytes 262176 | tf_op jit(solution)/shard_map/ppermute | solution.py:134
  259.1 8.9 %collective-permute-done.14.d2 = bf16[128,1024]{1,0:T(8,128)(2,1)S(1)} collective-permute-done((bf16[128,1024]{1,0:T(8,128)(2,1)S(1)}, bf16[128,1024]{1,0:T(8,128)(2,1)S(1)}, u32[]{:S(2)}, u32[]{:S(2)}) %collective-permute-start.14) | collective-permute-done | bytes 262176 | tf_op jit(solution)/shard_map/ppermute | solution.py:134
  268.0 1.3 collective-permute-start.15
  270.7 5.6 %collective-permute-done.15.d3 = bf16[128,1024]{1,0:T(8,128)(2,1)S(1)} collective-permute-done((bf16[128,1024]{1,0:T(8,128)(2,1)S(1)}, bf16[128,1024]{1,0:T(8,128)(2,1)S(1)}, u32[]{:S(2)}, u32[]{:S(2)}) %collective-permute-start.15) | collective-permute-done | bytes 262176 | tf_op jit(solution)/shard_map/ppermute | solution.py:134
  277.2 1.5 spread.1
  (76 shorter events, 19.5 us)
Async XLA Ops:
  8.1 25.9 %collective-permute-start.3 = (bf16[128,1024]{1,0:T(8,128)(2,1)S(1)}, bf16[128,1024]{1,0:T(8,128)(2,1)S(1)}, u32[]{:S(2)}, u32[]{:S(2)}) collective-permute-start(bf16[128,1024]{1,0:T(8,128)(2,1)S(1)} %constant_dynamic-slice_fusion), channel_id=1, source_target_pairs={{0,8},{8,0},{1,9},{9,1},{2,10},{10,2},{3,11},{11,3},{4,12},{12,4},... | collective-permute-start | bytes 786440 | tf_op jit(solution)/shard_map/ppermute | solution.py:458
  19.4 14.7 %all-to-all-start = ((s32[32,1,48]{2,1,0:T(1,128)}), s32[32,1,48]{2,1,0:T(1,128)S(1)}, u32[]{:S(2)}, u32[]{:S(2)}) async-start(s32[32,1,48]{2,1,0:T(1,128)} %bitcast.8), calls=%async_computation | async-start | bytes 32768 | tf_op jit(solution)/shard_map/all_to_all | solution.py:467
  28.7 5.6 %copy-start = (bf16[512,1024]{1,0:T(8,128)(2,1)S(1)}, bf16[512,1024]{1,0:T(8,128)(2,1)}, u32[]{:S(2)}) copy-start(bf16[512,1024]{1,0:T(8,128)(2,1)} %table_ref.1) | copy-start | bytes 3145732
  34.0 9.8 %copy-start.11 = (bf16[256,1280]{1,0:T(8,128)(2,1)}, bf16[256,1280]{1,0:T(8,128)(2,1)S(1)}, u32[]{:S(2)}) copy-start(bf16[256,1280]{1,0:T(8,128)(2,1)S(1)} %get-tuple-element.15.kv0_ref) | copy-start | bytes 1966084
  34.0 2.4 copy-start.19
  36.5 50.6 %all-to-all-start.1 = ((bf16[32,24,1024]{2,1,0:T(8,128)(2,1)}), bf16[32,24,1024]{2,1,0:T(8,128)(2,1)S(1)}, u32[]{:S(2)}, u32[]{:S(2)}) async-start(bf16[32,24,1024]{2,1,0:T(8,128)(2,1)} %bitcast.10), calls=%async_computation.1 | async-start | bytes 3145728 | tf_op jit(solution)/shard_map/all_to_all | solution.py:478
  43.9 18.0 %collective-permute-start = (bf16[256,1280]{1,0:T(8,128)(2,1)S(1)}, bf16[256,1280]{1,0:T(8,128)(2,1)}, u32[]{:S(2)}, u32[]{:S(2)}) collective-permute-start(bf16[256,1280]{1,0:T(8,128)(2,1)S(1)} %get-tuple-element.15.kv0_ref), channel_id=1, source_target_pairs={{0,64},{64,128},{128,192},{1,65},{65,129},{129,193},{2,66},{66,130... | collective-permute-start | bytes 1966088 | tf_op jit(solution)/shard_map/ppermute | solution.py:472
  47.7 19.6 %collective-permute-start.7 = (bf16[128,1024]{1,0:T(8,128)(2,1)S(1)}, bf16[128,1024]{1,0:T(8,128)(2,1)S(1)}, u32[]{:S(2)}, u32[]{:S(2)}) collective-permute-start(bf16[128,1024]{1,0:T(8,128)(2,1)S(1)} %collective-permute-done.3.own_ref), channel_id=1, source_target_pairs={{64,0},{128,64},{192,128},{65,1},{129,65},{193,129},{66,2},{130,66... | collective-permute-start | bytes 786440 | tf_op jit(solution)/shard_map/ppermute | solution.py:134
  49.0 19.6 %collective-permute-start.4 = (bf16[128,1024]{1,0:T(8,128)(2,1)S(1)}, bf16[128,1024]{1,0:T(8,128)(2,1)S(1)}, u32[]{:S(2)}, u32[]{:S(2)}) collective-permute-start(bf16[128,1024]{1,0:T(8,128)(2,1)S(1)} %collective-permute-done.3.own_ref), channel_id=1, source_target_pairs={{0,64},{64,128},{128,192},{1,65},{65,129},{129,193},{2,66},{66,130... | collective-permute-start | bytes 786440 | tf_op jit(solution)/shard_map/ppermute | solution.py:133
  61.9 19.0 %collective-permute-start.1 = (bf16[256,1280]{1,0:T(8,128)(2,1)}, bf16[256,1280]{1,0:T(8,128)(2,1)}, u32[]{:S(2)}, u32[]{:S(2)}) collective-permute-start(bf16[256,1280]{1,0:T(8,128)(2,1)} %collective-permute-done.kv1_ref), channel_id=1, source_target_pairs={{0,64},{64,128},{128,192},{1,65},{65,129},{129,193},{2,66},{66,130... | collective-permute-start | bytes 1966088 | tf_op jit(solution)/shard_map/ppermute | solution.py:472
  67.2 8.3 %collective-permute-start.8 = (bf16[128,1024]{1,0:T(8,128)(2,1)S(1)}, bf16[128,1024]{1,0:T(8,128)(2,1)S(1)}, u32[]{:S(2)}, u32[]{:S(2)}) collective-permute-start(bf16[128,1024]{1,0:T(8,128)(2,1)S(1)} %collective-permute-done.7.d1), channel_id=1, source_target_pairs={{64,0},{128,64},{65,1},{129,65},{66,2},{130,66},{67,3},{131,67},{6... | collective-permute-start | bytes 786440 | tf_op jit(solution)/shard_map/ppermute | solution.py:134
  68.5 8.3 %collective-permute-start.5 = (bf16[128,1024]{1,0:T(8,128)(2,1)S(1)}, bf16[128,1024]{1,0:T(8,128)(2,1)S(1)}, u32[]{:S(2)}, u32[]{:S(2)}) collective-permute-start(bf16[128,1024]{1,0:T(8,128)(2,1)S(1)} %collective-permute-done.4.u1), channel_id=1, source_target_pairs={{64,128},{128,192},{65,129},{129,193},{66,130},{130,194},{67,131},... | collective-permute-start | bytes 786440 | tf_op jit(solution)/shard_map/ppermute | solution.py:133
  75.6 8.3 %collective-permute-start.9 = (bf16[128,1024]{1,0:T(8,128)(2,1)S(1)}, bf16[128,1024]{1,0:T(8,128)(2,1)S(1)}, u32[]{:S(2)}, u32[]{:S(2)}) collective-permute-start(bf16[128,1024]{1,0:T(8,128)(2,1)S(1)} %collective-permute-done.8.d2), channel_id=1, source_target_pairs={{64,0},{65,1},{66,2},{67,3},{68,4},{69,5},{70,6},{71,7},{72,8},{73... | collective-permute-start | bytes 786440 | tf_op jit(solution)/shard_map/ppermute | solution.py:134
  76.9 7.0 %collective-permute-start.6 = (bf16[128,1024]{1,0:T(8,128)(2,1)S(1)}, bf16[128,1024]{1,0:T(8,128)(2,1)}, u32[]{:S(2)}, u32[]{:S(2)}) collective-permute-start(bf16[128,1024]{1,0:T(8,128)(2,1)S(1)} %collective-permute-done.5.u2), channel_id=1, source_target_pairs={{128,192},{129,193},{130,194},{131,195},{132,196},{133,197},{134,1... | collective-permute-start | bytes 786440 | tf_op jit(solution)/shard_map/ppermute | solution.py:133
  87.1 29.4 %copy-start.2 = (bf16[1,256,1024]{2,1,0:T(8,128)(2,1)S(1)}, bf16[1,256,1024]{2,1,0:T(8,128)(2,1)}, u32[]{:S(2)}) copy-start(bf16[1,256,1024]{2,1,0:T(8,128)(2,1)} %param.13) | copy-start | bytes 1572868
  87.1 29.4 %copy-start.10 = (bf16[256,1280]{1,0:T(8,128)(2,1)S(1)}, bf16[256,1280]{1,0:T(8,128)(2,1)}, u32[]{:S(2)}) copy-start(bf16[256,1280]{1,0:T(8,128)(2,1)} %copy-done.9) | copy-start | bytes 1966084
  87.1 29.4 %copy-start.15 = (f32[1024]{0:T(1024)S(1)}, f32[1024]{0:T(1024)}, u32[]{:S(2)}) copy-start(f32[1024]{0:T(1024)} %param.16) | copy-start | bytes 12292
  87.1 29.4 %copy-start.16 = (s32[1,3]{1,0:T(1,128)S(1)}, s32[1,3]{1,0:T(1,128)}, u32[]{:S(2)}) copy-start(s32[1,3]{1,0:T(1,128)} %len_ref.1) | copy-start | bytes 40
  87.1 36.1 %all-to-all-start.2 = ((bf16[32,24,1024]{2,1,0:T(8,128)(2,1)}), bf16[32,24,1024]{2,1,0:T(8,128)(2,1)}, u32[]{:S(2)}, u32[]{:S(2)}) async-start(bf16[32,24,1024]{2,1,0:T(8,128)(2,1)} %bitcast.12), calls=%async_computation.2 | async-start | bytes 3145728 | tf_op jit(solution)/shard_map/all_to_all | solution.py:480
  94.7 21.8 %collective-permute-start.2 = (bf16[256,1280]{1,0:T(8,128)(2,1)}, bf16[256,1280]{1,0:T(8,128)(2,1)}, u32[]{:S(2)}, u32[]{:S(2)}) collective-permute-start(bf16[256,1280]{1,0:T(8,128)(2,1)} %collective-permute-done.1.kv2_ref), channel_id=1, source_target_pairs={{0,64},{64,128},{128,192},{1,65},{65,129},{129,193},{2,66},{66,130... | collective-permute-start | bytes 1966088 | tf_op jit(solution)/shard_map/ppermute | solution.py:472
  117.6 5.6 %copy-start.13 = (f32[1024,8]{0,1:T(8,128)S(1)}, f32[1024,8]{0,1:T(8,128)}, u32[]{:S(2)}) copy-start(f32[1024,8]{0,1:T(8,128)} %param.19) | copy-start | bytes 98308
  117.6 5.6 %copy-start.14 = (f32[1024,8]{0,1:T(8,128)S(1)}, f32[1024,8]{0,1:T(8,128)}, u32[]{:S(2)}) copy-start(f32[1024,8]{0,1:T(8,128)} %param.20) | copy-start | bytes 98308
  144.1 8.2 %copy-start.20 = (s32[32,1,48]{2,1,0:T(1,128)S(1)}, s32[32,1,48]{2,1,0:T(1,128)}, u32[]{:S(2)}) copy-start(s32[32,1,48]{2,1,0:T(1,128)} %copy-done.19) | copy-start | bytes 18436
  144.1 45.3 %all-to-all-start.3 = ((bf16[32,48,1024]{2,1,0:T(8,128)(2,1)}), bf16[32,48,1024]{2,1,0:T(8,128)(2,1)S(1)}, u32[]{:S(2)}, u32[]{:S(2)}) async-start(bf16[32,48,1024]{2,1,0:T(8,128)(2,1)} %bitcast.32), calls=%async_computation.3 | async-start | bytes 6291456 | tf_op jit(solution)/shard_map/all_to_all | solution.py:486
  151.6 95.6 %reduce-scatter.2.cloned.1.call-start = ((), (), s32[]{:S(2)}) async-start(), calls=%async_computation.5 | async-start | bytes 2359296 | tf_op jit(solution)/shard_map/reduce_scatter | solution.py:490
  189.4 1.7 copy-start.18
  247.2 10.0 %collective-permute-start.13 = (bf16[128,1024]{1,0:T(8,128)(2,1)}, bf16[128,1024]{1,0:T(8,128)(2,1)S(1)}, u32[]{:S(2)}, u32[]{:S(2)}) collective-permute-start(bf16[128,1024]{1,0:T(8,128)(2,1)} %reduce-scatter.2.cloned.1.call-done.own_ref), channel_id=1, source_target_pairs={{64,0},{128,64},{192,128},{65,1},{129,65},{193,129},{66,2},{130,66... | collective-permute-start | bytes 786440 | tf_op jit(solution)/shard_map/ppermute | solution.py:134
  248.5 10.0 %collective-permute-start.10 = (bf16[128,1024]{1,0:T(8,128)(2,1)}, bf16[128,1024]{1,0:T(8,128)(2,1)S(1)}, u32[]{:S(2)}, u32[]{:S(2)}) collective-permute-start(bf16[128,1024]{1,0:T(8,128)(2,1)} %reduce-scatter.2.cloned.1.call-done.own_ref), channel_id=1, source_target_pairs={{0,64},{64,128},{128,192},{1,65},{65,129},{129,193},{2,66},{66,130... | collective-permute-start | bytes 786440 | tf_op jit(solution)/shard_map/ppermute | solution.py:133
  257.1 10.9 %collective-permute-start.14 = (bf16[128,1024]{1,0:T(8,128)(2,1)S(1)}, bf16[128,1024]{1,0:T(8,128)(2,1)S(1)}, u32[]{:S(2)}, u32[]{:S(2)}) collective-permute-start(bf16[128,1024]{1,0:T(8,128)(2,1)S(1)} %collective-permute-done.13.d1), channel_id=1, source_target_pairs={{64,0},{128,64},{65,1},{129,65},{66,2},{130,66},{67,3},{131,67},{6... | collective-permute-start | bytes 786440 | tf_op jit(solution)/shard_map/ppermute | solution.py:134
  258.4 10.9 %collective-permute-start.11 = (bf16[128,1024]{1,0:T(8,128)(2,1)S(1)}, bf16[128,1024]{1,0:T(8,128)(2,1)S(1)}, u32[]{:S(2)}, u32[]{:S(2)}) collective-permute-start(bf16[128,1024]{1,0:T(8,128)(2,1)S(1)} %collective-permute-done.10.u1), channel_id=1, source_target_pairs={{64,128},{128,192},{65,129},{129,193},{66,130},{130,194},{67,131},... | collective-permute-start | bytes 786440 | tf_op jit(solution)/shard_map/ppermute | solution.py:133
  268.0 8.3 %collective-permute-start.15 = (bf16[128,1024]{1,0:T(8,128)(2,1)S(1)}, bf16[128,1024]{1,0:T(8,128)(2,1)S(1)}, u32[]{:S(2)}, u32[]{:S(2)}) collective-permute-start(bf16[128,1024]{1,0:T(8,128)(2,1)S(1)} %collective-permute-done.14.d2), channel_id=1, source_target_pairs={{64,0},{65,1},{66,2},{67,3},{68,4},{69,5},{70,6},{71,7},{72,8},{73... | collective-permute-start | bytes 786440 | tf_op jit(solution)/shard_map/ppermute | solution.py:134
  269.3 7.0 %collective-permute-start.12 = (bf16[128,1024]{1,0:T(8,128)(2,1)S(1)}, bf16[128,1024]{1,0:T(8,128)(2,1)S(1)}, u32[]{:S(2)}, u32[]{:S(2)}) collective-permute-start(bf16[128,1024]{1,0:T(8,128)(2,1)S(1)} %collective-permute-done.11.u2), channel_id=1, source_target_pairs={{128,192},{129,193},{130,194},{131,195},{132,196},{133,197},{134,1... | collective-permute-start | bytes 786440 | tf_op jit(solution)/shard_map/ppermute | solution.py:133
  (10 other events, 8.6 us)
Sparse Core Ops, SparseCore 0:
  197.8 49.3 reduce-scatter.1

commit v2 on v1

--- a/solution.py
+++ b/solution.py
@@ -23,6 +23,8 @@
 PEERS = 32
 HALF_ROWS = PEERS * CAP
 QUARTER = ITEMS // 4
+WIDTHS = (512, 512)
+ATTEND_COST = 8 * 10**9
 QKW = 256
 PW = D // PARTS_SIZE
 TILE = 16
@@ -121,47 +123,28 @@
     rows_ref[...] = matmul(hot.astype(F32).astype(BF16), table_ref[...]).astype(BF16)
 
 
-def look(ids, table):
+def look(ids, table, cost=1):
     outs = jax.ShapeDtypeStruct((HALF_ROWS, D), BF16)
-    return vmem_call(look_body, outs, flops=2 * HALF_ROWS * ITEMS * D, moved=4 * 2**20, name="look")(ids, table)
+    return vmem_call(look_body, outs, flops=cost * 2 * HALF_ROWS * ITEMS * D, moved=4 * 2**20, name="look")(ids, table)
 
 
 def relay(own):
-    ups, downs = [], []
-    up = down = own
-    for hop in range(3):
-        up = lax.ppermute(up, "grp", [(i, i + 1) for i in range(hop, 3)])
-        down = lax.ppermute(down, "grp", [(i + 1, i) for i in range(3 - hop)])
-        ups.append(up)
-        downs.append(down)
-    return [own] + ups + downs
-
-
-def lay_out(grp, own_ref, up_refs, down_refs, out_ref):
-    def put(at, ref):
-        out_ref[pl.ds(pl.multiple_of(at * QUARTER, QUARTER), QUARTER), :] = ref[...].astype(out_ref.dtype)
-
-    put(grp, own_ref)
-    for k in range(3):
-        pl.when(grp > k)(lambda k=k: put(grp - k - 1, up_refs[k]))
-        pl.when(grp < 3 - k)(lambda k=k: put(grp + k + 1, down_refs[k]))
-
-
-def look_far_body(grp_ref, ids_ref, own_ref, u1, u2, u3, d1, d2, d3, rows_ref, table_ref):
-    lay_out(grp_ref[0], own_ref, (u1, u2, u3), (d1, d2, d3), table_ref)
-    look_body(ids_ref, table_ref, rows_ref)
-
-
-def look_far(grp, ids, quarters):
-    outs = jax.ShapeDtypeStruct((HALF_ROWS, D), BF16)
-    return vmem_call(
-        look_far_body, outs, n_smem=1, scratch=[pltpu.VMEM((ITEMS, D), BF16)], flops=2 * HALF_ROWS * ITEMS * D,
-        moved=4 * 2**20, name="look_far",
-    )(grp, ids, *quarters)
-
-
-def spread_body(grp_ref, own_ref, u1, u2, u3, d1, d2, d3, out_ref):
-    lay_out(grp_ref[0], own_ref, (u1, u2, u3), (d1, d2, d3), out_ref)
+    moved = [lax.ppermute(own, "grp", [(i, (i + k) % 4) for i in range(4)]) for k in (1, 2, 3)]
+    return [own] + moved
+
+
+def lay_out(grp, refs, out_ref, cols):
+    for k, ref in enumerate(refs):
+        at = ((grp - k) & 3) * QUARTER
+        out_ref[pl.ds(pl.multiple_of(at, QUARTER), QUARTER), cols] = ref[...].astype(out_ref.dtype)
+
+
+def spread_body(grp_ref, *refs):
+    out_ref = refs[-1]
+    at = 0
+    for i, width in enumerate(WIDTHS):
+        lay_out(grp_ref[0], refs[4 * i : 4 * i + 4], out_ref, slice(at, at + width))
+        at += width
 
 
 def spread(grp, quarters):
@@ -169,17 +152,45 @@
     return vmem_call(spread_body, outs, n_smem=1, moved=3 * 2**20, name="spread")(grp, *quarters)
 
 
-def add_body(ids_ref, grads_ref, table_ref):
-    for part in range(4):
-        size = 2 * ITEMS // 4
-        row = lax.broadcasted_iota(jnp.int32, (size, 2 * HALF_ROWS), 0) + part * size
+def add_body(place_ref, ids_ref, grads_ref, out_ref, *piece_refs):
+    eighth = 2 * ITEMS // 8
+    for pair in range(4):
+        row = lax.broadcasted_iota(jnp.int32, (2 * eighth, 2 * HALF_ROWS), 0) + pair * 2 * eighth
         hot = (ids_ref[...] == row).astype(F32).astype(BF16)
-        table_ref[part * size : (part + 1) * size, :] = matmul(hot, grads_ref[...]).astype(BF16)
-
-
-def add_up(ids, grads):
-    outs = jax.ShapeDtypeStruct((2 * ITEMS, D), BF16)
-    return vmem_call(add_body, outs, flops=8 * HALF_ROWS * ITEMS * D, moved=5 * 2**20, name="add_up")(ids, grads)
+        summed = matmul(hot, grads_ref[...]).astype(BF16)
+        for i in range(2):
+            k = 2 * pair + i
+            rows = slice(i * eighth, (i + 1) * eighth)
+            at = pl.multiple_of(((place_ref[0] + k) & 7) * eighth, eighth)
+            out_ref[pl.ds(at, eighth), :] = summed[rows, : WIDTHS[0]]
+            piece_refs[k][...] = summed[rows, WIDTHS[0] :]
+
+
+def add_up(place, ids, grads):
+    outs = (jax.ShapeDtypeStruct((2 * ITEMS, WIDTHS[0]), BF16),)
+    outs += (jax.ShapeDtypeStruct((ITEMS // 4, WIDTHS[1]), BF16),) * 8
+    return vmem_call(add_body, outs, n_smem=1, flops=8 * HALF_ROWS * ITEMS * D, moved=5 * 2**20, name="add_up")(
+        place, ids, grads
+    )
+
+
+def ring_sum(pieces):
+    def hop(value, step):
+        place = [(i % 4) * 2 + i // 4 for i in range(8)]
+        pairs = [(place[i], place[(i + step) % 8]) for i in range(8)]
+        return lax.ppermute(value, ("grp", "zh"), pairs)
+
+    def plus(value, piece):
+        return (value.astype(F32) + piece.astype(F32)).astype(BF16)
+
+    back = hop(pieces[4], -1)
+    ahead = hop(pieces[3], 1)
+    back = hop(plus(back, pieces[5]), -1)
+    ahead = hop(plus(ahead, pieces[2]), 1)
+    back = hop(plus(back, pieces[6]), -1)
+    ahead = hop(plus(ahead, pieces[1]), 1)
+    back = hop(plus(back, pieces[7]), -1)
+    return (pieces[0].astype(F32) + back.astype(F32) + ahead.astype(F32)).astype(BF16)
 
 
 def layer_norm(values, gain_vec):
@@ -244,7 +255,7 @@
 def attend(grp, lengths, own_tokens, gq, kvs, out_gain, w_out):
     outs = jax.ShapeDtypeStruct((TOK, D), F32)
     return vmem_call(
-        attend_body, outs, n_smem=2, scratch=[pltpu.VMEM((TOK, D), F32)], flops=2 * 10**9, moved=8 * 2**20, name="attend"
+        attend_body, outs, n_smem=2, scratch=[pltpu.VMEM((TOK, D), F32)], flops=ATTEND_COST, moved=8 * 2**20, name="attend"
     )(grp, lengths, own_tokens, gq, *kvs, out_gain, w_out)
 
 
@@ -453,10 +464,15 @@
     grp = lax.axis_index("grp").astype(jnp.int32)[None]
     barrier = lax.optimization_barrier
 
-    moved = lax.dynamic_slice_in_dim(item_table, grp[0] * QUARTER, QUARTER, 0)
-    half_then, _ = barrier((half, moved))
-    moved = lax.ppermute(moved, "zh", [(0, 1), (1, 0)])
-
+    quarter = lax.dynamic_slice_in_dim(item_table, grp[0] * QUARTER, QUARTER, 0)
+    tables = lax.all_gather(quarter, COLUMN, tiled=True)
+
+    gate_query, key_value = front_kernel(own_tokens, in_gain[None], w_in)
+    kvs = [key_value]
+    for _ in range(2):
+        kvs.append(lax.ppermute(kvs[-1], "grp", [(i, i + 1) for i in range(3)]))
+
+    half_then, _ = barrier((half, key_value))
     ask, place, back = pack(
         half_then,
         neg_owner.reshape(1, NEG),
@@ -466,29 +482,29 @@
     )
     asked = lax.all_to_all(ask, PLANE, split_axis=0, concat_axis=0, tiled=True)
 
-    gate_query, key_value = front_kernel(own_tokens, in_gain[None], w_in)
-    kvs = [key_value]
-    for hop in range(3):
-        kvs.append(lax.ppermute(kvs[-1], "grp", [(i, i + 1) for i in range(3)]))
-    quarters = relay(moved)
-
-    asked_then, _, _ = barrier((asked, key_value, moved))
+    asked_then, _ = barrier((asked, key_value))
     near_ids = asked_then[:, :CAP].reshape(-1, 1)
     far_ids = asked_then[:, CAP:].reshape(-1, 1)
     near = lax.all_to_all(look(near_ids, item_table), PLANE, split_axis=0, concat_axis=0, tiled=True)
-    far_ids, _ = barrier((far_ids, kvs[2]))
-    far = lax.all_to_all(look_far(grp, far_ids, quarters), PLANE, split_axis=0, concat_axis=0, tiled=True)
-
+    far_ids, _ = barrier((far_ids, kvs[1]))
+    far_table = lax.dynamic_slice_in_dim(tables, (1 - half[0]) * ITEMS, ITEMS, 0)
+    looked = look(far_ids, far_table, 20)
+    far = lax.all_to_all(looked, PLANE, split_axis=0, concat_axis=0, tiled=True)
+
+    kvs[2], _ = barrier((kvs[2], looked))
+    kvs.append(lax.ppermute(kvs[2], "grp", [(i, i + 1) for i in range(3)]))
     query = attend(grp, lengths, own_tokens, gate_query, kvs, out_gain[None], w_out)
 
     losses, query_grad, grads = loss_and_grads(query, near, far, place, back, w_qgate, w_xgate)
 
     came = lax.all_to_all(grads, PLANE, split_axis=0, concat_axis=0, tiled=True)
     shard = half[0] ^ (lax.broadcasted_iota(jnp.int32, asked.shape, 1) // CAP)
-    rows = jnp.where(asked >= 0, asked + shard * ITEMS, -1).reshape(1, -1)
-    table = add_up(rows, came)
-    table = lax.psum_scatter(table, COLUMN, tiled=True)
-    return (losses.reshape(1, TOK), query_grad[None], spread(grp, relay(table)))
+    at = half * 4 + grp
+    row = (asked + shard * ITEMS - at[0] * QUARTER) & (2 * ITEMS - 1)
+    first, *pieces = add_up(at, jnp.where(asked >= 0, row, -1).reshape(1, -1), came)
+    first = lax.psum_scatter(first, COLUMN, tiled=True)
+    rest = ring_sum(pieces)
+    return (losses.reshape(1, TOK), query_grad[None], spread(grp, relay(first) + relay(rest)))
 
 
 def solution(mesh):

time: 287 us -> 240 us (0.84); the launches traced: 286 us -> 235 us
  waiting for transfers between devices: 138 us -> 101 us
  starting transfers between devices: 74.8 us -> 66.5 us
  local copies, waits for them, and re-layouts: 12.6 us -> 9.31 us
    reduce_scatter x1, waiting for transfers between devices: 49.5 us -> 8.16 us  [local(): first = lax.psum_scatter(first, COLUMN, tiled=True)]
    ppermute x3 -> x2, waiting for transfers between devices: 24.4 us -> 0.03 us  [local(): kvs.append(lax.ppermute(kvs[-1], 'grp', [(i, i + 1) for i in range(3)]))]
    all_gather x0 -> x1, waiting for transfers between devices: none -> 14.6 us  [local(): tables = lax.all_gather(quarter, COLUMN, tiled=True)]
    ppermute x13 -> x14, waiting for transfers between devices: 27.8 us -> 36.5 us  [the longest x7 14.9 us: hop(): return lax.ppermute(value, ('grp', 'zh'), pairs)]
    ppermute x3 -> x2, starting transfers between devices: 17.1 us -> 10.1 us  [local(): kvs.append(lax.ppermute(kvs[-1], 'grp', [(i, i + 1) for i in range(3)]))]
    unnamed x42 -> x32, local copies, waits for them, and re-layouts: 10.2 us -> 4.98 us
    all_to_all x1, waiting for transfers between devices: 0.01 us -> 5.14 us  [local(): asked = lax.all_to_all(ask, PLANE, split_axis=0, concat_axis=0, tiled=True)]
    ppermute x13 -> x14, starting transfers between devices: 27.5 us -> 27.3 us  [the longest x7 14.6 us: hop(): return lax.ppermute(value, ('grp', 'zh'), pairs)]
  transfers between devices with their start and end apart: 21 -> 22, of which waited for: 10 -> 13; matrix products, arithmetic and copies ran while one was open for 1% -> 2% of each run, Pallas kernels for 5% -> 7%
where the time goes in v2:
time: 240 us; the launch traced here: 235 us
  waiting for transfers between devices  101 us (42%)
  starting transfers between devices  66.5 us (28%)
  Pallas kernels  42.6 us (18%)
  between operations  14.3 us (6%)
  local copies, waits for them, and re-layouts  9.31 us (4%)
    pallas_call x8, Pallas kernels, call(): pl.pallas_call(body, out_shape=outs, in_specs=in_specs, out_specs=jax.tre...  42.6 us
    all_to_all x1, waiting for transfers between devices, local(): came = lax.all_to_all(grads, PLANE, split_axis=0, concat_axis=0, tiled=True)  36.3 us
    ppermute x7, waiting for transfers between devices, hop(): return lax.ppermute(value, ('grp', 'zh'), pairs)  14.9 us
    all_gather x1, waiting for transfers between devices, local(): tables = lax.all_gather(quarter, COLUMN, tiled=True)  14.6 us
    ppermute x7, starting transfers between devices, hop(): return lax.ppermute(value, ('grp', 'zh'), pairs)  14.6 us
    ppermute x1, waiting for transfers between devices, local(): kvs.append(lax.ppermute(kvs[2], 'grp', [(i, i + 1) for i in range(3)]))  13.6 us
    ppermute x2, starting transfers between devices, local(): kvs.append(lax.ppermute(kvs[-1], 'grp', [(i, i + 1) for i in range(3)]))  10.1 us
    reduce_scatter x1, waiting for transfers between devices, local(): first = lax.psum_scatter(first, COLUMN, tiled=True)  8.16 us
  transfers between devices with their start and end apart: 22, of which 13 were waited for; matrix products, arithmetic and copies ran while one was open for 2% of the time, Pallas kernels for 7%

profile of v2, /device:TPU:4, one launch (start us, length us, event | category | flops | bytes accessed | tf_op | source)
XLA Modules:
  0.0 235.1 jit_solution(11870909215424259118)
XLA Ops:
  7.2 1.7 constant_dynamic-slice_fusion.1
  10.7 4.5 %front.1 = (bf16[256,1280]{1,0:T(8,128)(2,1)S(1)}, bf16[256,1280]{1,0:T(8,128)(2,1)S(1)}) custom-call(bf16[256,1024]{1,0:T(8,128)(2,1)S(1)} %bitcast.24, f32[1,1024]{1,0:T(1,128)S(1)} %bitcast.26, bf16[1024,2560]{1,0:T(8,128)(2,1)} %w_ref.1), custom_call_target="tpu_custom_call" | custom-call | flops 1400000000 | bytes 7340032 | tf_op jit(solution)/shard_map/front/pallas_call | solution.py:58
  15.2 4.7 %collective-permute-start = (bf16[256,1280]{1,0:T(8,128)(2,1)S(1)}, bf16[256,1280]{1,0:T(8,128)(2,1)}, u32[]{:S(2)}, u32[]{:S(2)}) collective-permute-start(bf16[256,1280]{1,0:T(8,128)(2,1)S(1)} %get-tuple-element.25.kv0_ref), channel_id=1, source_target_pairs={{0,64},{64,128},{128,192},{1,65},{65,129},{129,193},{2,66},{66,130... | collective-permute-start | bytes 1966088 | tf_op jit(solution)/shard_map/ppermute | solution.py:473
  21.1 7.6 %all-to-all-start = ((s32[32,1,48]{2,1,0:T(1,128)}), s32[32,1,48]{2,1,0:T(1,128)S(1)}, u32[]{:S(2)}, u32[]{:S(2)}) async-start(s32[32,1,48]{2,1,0:T(1,128)} %bitcast.7), calls=%async_computation | async-start | bytes 32768 | tf_op jit(solution)/shard_map/all_to_all | solution.py:483
  28.7 5.1 %all-to-all-done = s32[32,1,48]{2,1,0:T(1,128)S(1)} async-done(((s32[32,1,48]{2,1,0:T(1,128)}), s32[32,1,48]{2,1,0:T(1,128)S(1)}, u32[]{:S(2)}, u32[]{:S(2)}) %all-to-all-start) | async-done | bytes 6176 | tf_op jit(solution)/shard_map/all_to_all | solution.py:483
  34.2 2.2 look.3
  36.4 6.0 %all-to-all-start.1 = ((bf16[32,24,1024]{2,1,0:T(8,128)(2,1)}), bf16[32,24,1024]{2,1,0:T(8,128)(2,1)S(1)}, u32[]{:S(2)}, u32[]{:S(2)}) async-start(bf16[32,24,1024]{2,1,0:T(8,128)(2,1)} %bitcast.10), calls=%async_computation.1 | async-start | bytes 3145728 | tf_op jit(solution)/shard_map/all_to_all | solution.py:488
  42.6 5.3 %collective-permute-start.1 = (bf16[256,1280]{1,0:T(8,128)(2,1)}, bf16[256,1280]{1,0:T(8,128)(2,1)}, u32[]{:S(2)}, u32[]{:S(2)}) collective-permute-start(bf16[256,1280]{1,0:T(8,128)(2,1)} %collective-permute-done.kv1_ref), channel_id=1, source_target_pairs={{0,64},{64,128},{128,192},{1,65},{65,129},{129,193},{2,66},{66,130... | collective-permute-start | bytes 1966088 | tf_op jit(solution)/shard_map/ppermute | solution.py:473
  48.0 14.6 %all-gather.2.cloned.1.call-done = bf16[1024,1024]{1,0:T(8,128)(2,1)} async-done(((bf16[128,1024]{1,0:T(8,128)(2,1)}), bf16[1024,1024]{1,0:T(8,128)(2,1)}) %all-gather.2.cloned.1.call-update) | async-done | bytes 2097168 | tf_op jit(solution)/shard_map/all_gather | solution.py:468
  63.9 2.2 look.2
  66.1 8.0 %all-to-all-start.2 = ((bf16[32,24,1024]{2,1,0:T(8,128)(2,1)}), bf16[32,24,1024]{2,1,0:T(8,128)(2,1)}, u32[]{:S(2)}, u32[]{:S(2)}) async-start(bf16[32,24,1024]{2,1,0:T(8,128)(2,1)} %bitcast.12), calls=%async_computation.2 | async-start | bytes 3145728 | tf_op jit(solution)/shard_map/all_to_all | solution.py:492
  74.1 5.4 %collective-permute-start.2 = (bf16[256,1280]{1,0:T(8,128)(2,1)}, bf16[256,1280]{1,0:T(8,128)(2,1)}, u32[]{:S(2)}, u32[]{:S(2)}) collective-permute-start(bf16[256,1280]{1,0:T(8,128)(2,1)} %collective-permute-done.1.kv2_ref), channel_id=1, source_target_pairs={{0,64},{64,128},{128,192},{1,65},{65,129},{129,193},{2,66},{66,130... | collective-permute-start | bytes 1966088 | tf_op jit(solution)/shard_map/ppermute | solution.py:495
  79.7 13.6 %collective-permute-done.2.kv3_ref = bf16[256,1280]{1,0:T(8,128)(2,1)} collective-permute-done((bf16[256,1280]{1,0:T(8,128)(2,1)}, bf16[256,1280]{1,0:T(8,128)(2,1)}, u32[]{:S(2)}, u32[]{:S(2)}) %collective-permute-start.2) | collective-permute-done | bytes 655392 | tf_op jit(solution)/shard_map/ppermute | solution.py:495
  94.4 5.6 %attend.1.query_ref = f32[256,1024]{1,0:T(8,128)} custom-call(s32[1]{0:T(128)} %bitcast.grp_ref, s32[1,3]{1,0:T(1,128)S(1)} %copy-done.14, bf16[256,1024]{1,0:T(8,128)(2,1)S(1)} %bitcast.25, bf16[256,1280]{1,0:T(8,128)(2,1)S(1)} %get-tuple-element.24.gq_ref, bf16[256,1280]{1,0:T(8,128)(2,1)S(1)} %copy-done.10, ...), custom_call_target="tpu_custom_call" | custom-call | flops 8000000000 | bytes 8388608 | tf_op jit(solution)/shard_map/attend/pallas_call | solution.py:58
  101.2 19.6 %loss.1 = (f32[256,1]{1,0:T(8,128)S(1)}, bf16[256,1024]{1,0:T(8,128)(2,1)}, bf16[1536,1024]{1,0:T(8,128)(2,1)}) custom-call(f32[256,1024]{1,0:T(8,128)S(1)} %copy-done.15, bf16[768,1024]{1,0:T(8,128)(2,1)S(1)} %bitcast.23, bf16[768,1024]{1,0:T(8,128)(2,1)} %bitcast.13.far_ref, s32[768,1]{1,0:T(8,128)S(1)} %copy.22.place_ref, ...), custom_call_target="tpu_custom_call" | custom-call | flops 8000000000 | bytes 10485760 | tf_op jit(solution)/shard_map/loss/pallas_call | solution.py:58
  120.8 7.4 %all-to-all-start.3 = ((bf16[32,48,1024]{2,1,0:T(8,128)(2,1)}), bf16[32,48,1024]{2,1,0:T(8,128)(2,1)}, u32[]{:S(2)}, u32[]{:S(2)}) async-start(bf16[32,48,1024]{2,1,0:T(8,128)(2,1)} %bitcast.33), calls=%async_computation.3 | async-start | bytes 6291456 | tf_op jit(solution)/shard_map/all_to_all | solution.py:500
  129.7 36.3 %all-to-all-done.3 = bf16[32,48,1024]{2,1,0:T(8,128)(2,1)} async-done(((bf16[32,48,1024]{2,1,0:T(8,128)(2,1)}), bf16[32,48,1024]{2,1,0:T(8,128)(2,1)}, u32[]{:S(2)}, u32[]{:S(2)}) %all-to-all-start.3) | async-done | bytes 3145760 | tf_op jit(solution)/shard_map/all_to_all | solution.py:500
  166.0 5.9 %add_up.1 = (bf16[1024,512]{1,0:T(8,128)(2,1)}, bf16[128,512]{1,0:T(8,128)(2,1)S(1)}, bf16[128,512]{1,0:T(8,128)(2,1)S(1)}, bf16[128,512]{1,0:T(8,128)(2,1)S(1)}...) custom-call(s32[1]{0:T(128)S(6)} %add.46.place_ref, ...), custom_call_target="tpu_custom_call" | custom-call | flops 3221225472 | bytes 5242880 | tf_op jit(solution)/shard_map/add_up/pallas_call | solution.py:58
  171.9 3.1 %collective-permute-start.6 = (bf16[128,512]{1,0:T(8,128)(2,1)S(1)}, bf16[128,512]{1,0:T(8,128)(2,1)S(1)}, u32[]{:S(2)}, u32[]{:S(2)}) collective-permute-start(bf16[128,512]{1,0:T(8,128)(2,1)S(1)} %get-tuple-element.38), channel_id=1, source_target_pairs={{0,200},{64,0},{128,64},{192,128},{8,192},{72,8},{136,72},{200,136... | collective-permute-start | bytes 393224 | tf_op jit(solution)/shard_map/ppermute | solution.py:181
  175.0 3.2 %collective-permute-done.6 = bf16[128,512]{1,0:T(8,128)(2,1)S(1)} collective-permute-done((bf16[128,512]{1,0:T(8,128)(2,1)S(1)}, bf16[128,512]{1,0:T(8,128)(2,1)S(1)}, u32[]{:S(2)}, u32[]{:S(2)}) %collective-permute-start.6) | collective-permute-done | bytes 131104 | tf_op jit(solution)/shard_map/ppermute | solution.py:181
  178.3 3.8 %collective-permute-start.7 = (bf16[128,512]{1,0:T(8,128)(2,1)S(1)}, bf16[128,512]{1,0:T(8,128)(2,1)S(1)}, u32[]{:S(2)}, u32[]{:S(2)}) collective-permute-start(bf16[128,512]{1,0:T(8,128)(2,1)S(1)} %add_convert_fusion.5), channel_id=1, source_target_pairs={{0,200},{64,0},{128,64},{192,128},{8,192},{72,8},{136,72},{200,136... | collective-permute-start | bytes 393224 | tf_op jit(solution)/shard_map/ppermute | solution.py:181
  182.2 3.4 %collective-permute-done.7 = bf16[128,512]{1,0:T(8,128)(2,1)S(1)} collective-permute-done((bf16[128,512]{1,0:T(8,128)(2,1)S(1)}, bf16[128,512]{1,0:T(8,128)(2,1)S(1)}, u32[]{:S(2)}, u32[]{:S(2)}) %collective-permute-start.7) | collective-permute-done | bytes 131104 | tf_op jit(solution)/shard_map/ppermute | solution.py:181
  185.7 3.8 %collective-permute-start.8 = (bf16[128,512]{1,0:T(8,128)(2,1)S(1)}, bf16[128,512]{1,0:T(8,128)(2,1)S(1)}, u32[]{:S(2)}, u32[]{:S(2)}) collective-permute-start(bf16[128,512]{1,0:T(8,128)(2,1)S(1)} %add_convert_fusion.4), channel_id=1, source_target_pairs={{0,200},{64,0},{128,64},{192,128},{8,192},{72,8},{136,72},{200,136... | collective-permute-start | bytes 393224 | tf_op jit(solution)/shard_map/ppermute | solution.py:181
  189.8 4.0 %collective-permute-done.8 = bf16[128,512]{1,0:T(8,128)(2,1)S(1)} collective-permute-done((bf16[128,512]{1,0:T(8,128)(2,1)S(1)}, bf16[128,512]{1,0:T(8,128)(2,1)S(1)}, u32[]{:S(2)}, u32[]{:S(2)}) %collective-permute-start.8) | collective-permute-done | bytes 131104 | tf_op jit(solution)/shard_map/ppermute | solution.py:181
  193.9 3.8 %collective-permute-start.9 = (bf16[128,512]{1,0:T(8,128)(2,1)S(1)}, bf16[128,512]{1,0:T(8,128)(2,1)S(1)}, u32[]{:S(2)}, u32[]{:S(2)}) collective-permute-start(bf16[128,512]{1,0:T(8,128)(2,1)S(1)} %add_convert_fusion.3), channel_id=1, source_target_pairs={{0,200},{64,0},{128,64},{192,128},{8,192},{72,8},{136,72},{200,136... | collective-permute-start | bytes 393224 | tf_op jit(solution)/shard_map/ppermute | solution.py:181
  197.6 4.0 %collective-permute-done.9 = bf16[128,512]{1,0:T(8,128)(2,1)S(1)} collective-permute-done((bf16[128,512]{1,0:T(8,128)(2,1)S(1)}, bf16[128,512]{1,0:T(8,128)(2,1)S(1)}, u32[]{:S(2)}, u32[]{:S(2)}) %collective-permute-start.9) | collective-permute-done | bytes 131104 | tf_op jit(solution)/shard_map/ppermute | solution.py:181
  202.1 1.7 collective-permute-start.13
  203.8 8.2 %reduce-scatter.2.cloned.1.call-done.refs_0_ = bf16[128,512]{1,0:T(8,128)(2,1)} async-done(((bf16[1024,512]{1,0:T(8,128)(2,1)}), bf16[128,512]{1,0:T(8,128)(2,1)}) %reduce-scatter.2.cloned.1.call-update) | async-done | bytes 131088 | tf_op jit(solution)/shard_map/reduce_scatter | solution.py:505
  211.9 4.0 %collective-permute-start.5 = (bf16[128,512]{1,0:T(8,128)(2,1)}, bf16[128,512]{1,0:T(8,128)(2,1)S(1)}, u32[]{:S(2)}, u32[]{:S(2)}) collective-permute-start(bf16[128,512]{1,0:T(8,128)(2,1)} %reduce-scatter.2.cloned.1.call-done.refs_0_), channel_id=1, source_target_pairs={{0,192},{64,0},{128,64},{192,128},{1,193},{65,1},{129,65},{193,129... | collective-permute-start | bytes 393224 | tf_op jit(solution)/shard_map/ppermute | solution.py:132
  218.3 1.9 collective-permute-done.5.refs_3_
  220.2 5.6 %collective-permute-done.4.refs_2_ = bf16[128,512]{1,0:T(8,128)(2,1)S(1)} collective-permute-done((bf16[128,512]{1,0:T(8,128)(2,1)}, bf16[128,512]{1,0:T(8,128)(2,1)S(1)}, u32[]{:S(2)}, u32[]{:S(2)}) %collective-permute-start.4) | collective-permute-done | bytes 131104 | tf_op jit(solution)/shard_map/ppermute | solution.py:132
  226.8 1.5 spread.1
  (76 shorter events, 13.2 us)
Async XLA Ops:
  7.2 55.4 %all-gather.2.cloned.1.call-start = ((), (), s32[]{:S(2)}) async-start(), calls=%async_computation.5 | async-start | bytes 2359296 | tf_op jit(solution)/shard_map/all_gather | solution.py:468
  10.6 9.2 %copy-start.5 = (s32[1,512,1]{1,2,0:T(1,128)S(1)}, s32[1,512,1]{1,2,0:T(1,128)}, u32[]{:S(2)}) copy-start(s32[1,512,1]{1,2,0:T(1,128)} %param.22) | copy-start | bytes 6148
  10.6 9.2 %copy-start.6 = (s32[1,512]{1,0:T(1,128)S(1)}, s32[1,512]{1,0:T(1,128)}, u32[]{:S(2)}) copy-start(s32[1,512]{1,0:T(1,128)} %nslot_ref.1) | copy-start | bytes 6148
  10.7 9.2 %copy-start.7 = (s32[1,256,1]{1,2,0:T(1,128)S(1)}, s32[1,256,1]{1,2,0:T(1,128)}, u32[]{:S(2)}) copy-start(s32[1,256,1]{1,2,0:T(1,128)} %param.24) | copy-start | bytes 3076
  10.7 9.2 %copy-start.8 = (s32[1,256]{1,0:T(1,128)S(1)}, s32[1,256]{1,0:T(1,128)}, u32[]{:S(2)}) copy-start(s32[1,256]{1,0:T(1,128)} %pslot_ref.1) | copy-start | bytes 3076
  10.7 23.6 %copy-start = (bf16[512,1024]{1,0:T(8,128)(2,1)S(1)}, bf16[512,1024]{1,0:T(8,128)(2,1)}, u32[]{:S(2)}) copy-start(bf16[512,1024]{1,0:T(8,128)(2,1)} %table_ref.1) | copy-start | bytes 3145732
  15.2 21.2 %copy-start.9 = (bf16[256,1280]{1,0:T(8,128)(2,1)}, bf16[256,1280]{1,0:T(8,128)(2,1)S(1)}, u32[]{:S(2)}) copy-start(bf16[256,1280]{1,0:T(8,128)(2,1)S(1)} %get-tuple-element.25.kv0_ref) | copy-start | bytes 1966084
  15.2 27.3 %collective-permute-start = (bf16[256,1280]{1,0:T(8,128)(2,1)S(1)}, bf16[256,1280]{1,0:T(8,128)(2,1)}, u32[]{:S(2)}, u32[]{:S(2)}) collective-permute-start(bf16[256,1280]{1,0:T(8,128)(2,1)S(1)} %get-tuple-element.25.kv0_ref), channel_id=1, source_target_pairs={{0,64},{64,128},{128,192},{1,65},{65,129},{129,193},{2,66},{66,130... | collective-permute-start | bytes 1966088 | tf_op jit(solution)/shard_map/ppermute | solution.py:473
  21.1 12.8 %all-to-all-start = ((s32[32,1,48]{2,1,0:T(1,128)}), s32[32,1,48]{2,1,0:T(1,128)S(1)}, u32[]{:S(2)}, u32[]{:S(2)}) async-start(s32[32,1,48]{2,1,0:T(1,128)} %bitcast.7), calls=%async_computation | async-start | bytes 32768 | tf_op jit(solution)/shard_map/all_to_all | solution.py:483
  36.4 29.7 %all-to-all-start.1 = ((bf16[32,24,1024]{2,1,0:T(8,128)(2,1)}), bf16[32,24,1024]{2,1,0:T(8,128)(2,1)S(1)}, u32[]{:S(2)}, u32[]{:S(2)}) async-start(bf16[32,24,1024]{2,1,0:T(8,128)(2,1)} %bitcast.10), calls=%async_computation.1 | async-start | bytes 3145728 | tf_op jit(solution)/shard_map/all_to_all | solution.py:488
  42.6 31.5 %collective-permute-start.1 = (bf16[256,1280]{1,0:T(8,128)(2,1)}, bf16[256,1280]{1,0:T(8,128)(2,1)}, u32[]{:S(2)}, u32[]{:S(2)}) collective-permute-start(bf16[256,1280]{1,0:T(8,128)(2,1)} %collective-permute-done.kv1_ref), channel_id=1, source_target_pairs={{0,64},{64,128},{128,192},{1,65},{65,129},{129,193},{2,66},{66,130... | collective-permute-start | bytes 1966088 | tf_op jit(solution)/shard_map/ppermute | solution.py:473
  66.1 27.2 %copy-start.2 = (bf16[1,256,1024]{2,1,0:T(8,128)(2,1)S(1)}, bf16[1,256,1024]{2,1,0:T(8,128)(2,1)}, u32[]{:S(2)}) copy-start(bf16[1,256,1024]{2,1,0:T(8,128)(2,1)} %param.13) | copy-start | bytes 1572868
  66.1 27.2 %copy-start.13 = (f32[1024]{0:T(1024)S(1)}, f32[1024]{0:T(1024)}, u32[]{:S(2)}) copy-start(f32[1024]{0:T(1024)} %param.16) | copy-start | bytes 12292
  66.1 27.2 %copy-start.14 = (s32[1,3]{1,0:T(1,128)S(1)}, s32[1,3]{1,0:T(1,128)}, u32[]{:S(2)}) copy-start(s32[1,3]{1,0:T(1,128)} %len_ref.1) | copy-start | bytes 40
  66.1 33.9 %all-to-all-start.2 = ((bf16[32,24,1024]{2,1,0:T(8,128)(2,1)}), bf16[32,24,1024]{2,1,0:T(8,128)(2,1)}, u32[]{:S(2)}, u32[]{:S(2)}) async-start(bf16[32,24,1024]{2,1,0:T(8,128)(2,1)} %bitcast.12), calls=%async_computation.2 | async-start | bytes 3145728 | tf_op jit(solution)/shard_map/all_to_all | solution.py:492
  74.1 19.2 %collective-permute-start.2 = (bf16[256,1280]{1,0:T(8,128)(2,1)}, bf16[256,1280]{1,0:T(8,128)(2,1)}, u32[]{:S(2)}, u32[]{:S(2)}) collective-permute-start(bf16[256,1280]{1,0:T(8,128)(2,1)} %collective-permute-done.1.kv2_ref), channel_id=1, source_target_pairs={{0,64},{64,128},{128,192},{1,65},{65,129},{129,193},{2,66},{66,130... | collective-permute-start | bytes 1966088 | tf_op jit(solution)/shard_map/ppermute | solution.py:495
  94.4 5.6 %copy-start.12 = (f32[1024,8]{0,1:T(8,128)S(1)}, f32[1024,8]{0,1:T(8,128)}, u32[]{:S(2)}) copy-start(f32[1024,8]{0,1:T(8,128)} %param.20) | copy-start | bytes 98308
  120.8 45.3 %all-to-all-start.3 = ((bf16[32,48,1024]{2,1,0:T(8,128)(2,1)}), bf16[32,48,1024]{2,1,0:T(8,128)(2,1)}, u32[]{:S(2)}, u32[]{:S(2)}) async-start(bf16[32,48,1024]{2,1,0:T(8,128)(2,1)} %bitcast.33), calls=%async_computation.3 | async-start | bytes 6291456 | tf_op jit(solution)/shard_map/all_to_all | solution.py:500
  128.2 83.7 %reduce-scatter.2.cloned.1.call-start = ((), (), s32[]{:S(2)}) async-start(), calls=%async_computation.6 | async-start | bytes 1179648 | tf_op jit(solution)/shard_map/reduce_scatter | solution.py:505
  171.9 6.3 %collective-permute-start.6 = (bf16[128,512]{1,0:T(8,128)(2,1)S(1)}, bf16[128,512]{1,0:T(8,128)(2,1)S(1)}, u32[]{:S(2)}, u32[]{:S(2)}) collective-permute-start(bf16[128,512]{1,0:T(8,128)(2,1)S(1)} %get-tuple-element.38), channel_id=1, source_target_pairs={{0,200},{64,0},{128,64},{192,128},{8,192},{72,8},{136,72},{200,136... | collective-permute-start | bytes 393224 | tf_op jit(solution)/shard_map/ppermute | solution.py:181
  175.0 7.1 %collective-permute-start.10 = (bf16[128,512]{1,0:T(8,128)(2,1)S(1)}, bf16[128,512]{1,0:T(8,128)(2,1)S(1)}, u32[]{:S(2)}, u32[]{:S(2)}) collective-permute-start(bf16[128,512]{1,0:T(8,128)(2,1)S(1)} %get-tuple-element.42), channel_id=1, source_target_pairs={{0,64},{64,128},{128,192},{192,8},{8,72},{72,136},{136,200},{200,0... | collective-permute-start | bytes 393224 | tf_op jit(solution)/shard_map/ppermute | solution.py:181
  178.3 7.4 %collective-permute-start.7 = (bf16[128,512]{1,0:T(8,128)(2,1)S(1)}, bf16[128,512]{1,0:T(8,128)(2,1)S(1)}, u32[]{:S(2)}, u32[]{:S(2)}) collective-permute-start(bf16[128,512]{1,0:T(8,128)(2,1)S(1)} %add_convert_fusion.5), channel_id=1, source_target_pairs={{0,200},{64,0},{128,64},{192,128},{8,192},{72,8},{136,72},{200,136... | collective-permute-start | bytes 393224 | tf_op jit(solution)/shard_map/ppermute | solution.py:181
  182.1 7.6 %collective-permute-start.11 = (bf16[128,512]{1,0:T(8,128)(2,1)S(1)}, bf16[128,512]{1,0:T(8,128)(2,1)S(1)}, u32[]{:S(2)}, u32[]{:S(2)}) collective-permute-start(bf16[128,512]{1,0:T(8,128)(2,1)S(1)} %add_convert_fusion.2), channel_id=1, source_target_pairs={{0,64},{64,128},{128,192},{192,8},{8,72},{72,136},{136,200},{200,0... | collective-permute-start | bytes 393224 | tf_op jit(solution)/shard_map/ppermute | solution.py:181
  185.7 8.2 %collective-permute-start.8 = (bf16[128,512]{1,0:T(8,128)(2,1)S(1)}, bf16[128,512]{1,0:T(8,128)(2,1)S(1)}, u32[]{:S(2)}, u32[]{:S(2)}) collective-permute-start(bf16[128,512]{1,0:T(8,128)(2,1)S(1)} %add_convert_fusion.4), channel_id=1, source_target_pairs={{0,200},{64,0},{128,64},{192,128},{8,192},{72,8},{136,72},{200,136... | collective-permute-start | bytes 393224 | tf_op jit(solution)/shard_map/ppermute | solution.py:181
  189.8 7.9 %collective-permute-start.12 = (bf16[128,512]{1,0:T(8,128)(2,1)S(1)}, bf16[128,512]{1,0:T(8,128)(2,1)S(1)}, u32[]{:S(2)}, u32[]{:S(2)}) collective-permute-start(bf16[128,512]{1,0:T(8,128)(2,1)S(1)} %add_convert_fusion.1), channel_id=1, source_target_pairs={{0,64},{64,128},{128,192},{192,8},{8,72},{72,136},{136,200},{200,0... | collective-permute-start | bytes 393224 | tf_op jit(solution)/shard_map/ppermute | solution.py:181
  193.9 7.7 %collective-permute-start.9 = (bf16[128,512]{1,0:T(8,128)(2,1)S(1)}, bf16[128,512]{1,0:T(8,128)(2,1)S(1)}, u32[]{:S(2)}, u32[]{:S(2)}) collective-permute-start(bf16[128,512]{1,0:T(8,128)(2,1)S(1)} %add_convert_fusion.3), channel_id=1, source_target_pairs={{0,200},{64,0},{128,64},{192,128},{8,192},{72,8},{136,72},{200,136... | collective-permute-start | bytes 393224 | tf_op jit(solution)/shard_map/ppermute | solution.py:181
  201.7 15.5 %collective-permute-start.15 = (bf16[128,512]{1,0:T(8,128)(2,1)S(1)}, bf16[128,512]{1,0:T(8,128)(2,1)S(1)}, u32[]{:S(2)}, u32[]{:S(2)}) collective-permute-start(bf16[128,512]{1,0:T(8,128)(2,1)S(1)} %add_convert_fusion.refs_4_), channel_id=1, source_target_pairs={{0,192},{64,0},{128,64},{192,128},{1,193},{65,1},{129,65},{193,129... | collective-permute-start | bytes 393224 | tf_op jit(solution)/shard_map/ppermute | solution.py:132
  202.1 16.2 %collective-permute-start.14 = (bf16[128,512]{1,0:T(8,128)(2,1)S(1)}, bf16[128,512]{1,0:T(8,128)(2,1)S(1)}, u32[]{:S(2)}, u32[]{:S(2)}) collective-permute-start(bf16[128,512]{1,0:T(8,128)(2,1)S(1)} %add_convert_fusion.refs_4_), channel_id=1, source_target_pairs={{0,128},{64,192},{128,0},{192,64},{1,129},{65,193},{129,1},{193,65... | collective-permute-start | bytes 393224 | tf_op jit(solution)/shard_map/ppermute | solution.py:132
  202.1 16.2 %collective-permute-start.13 = (bf16[128,512]{1,0:T(8,128)(2,1)S(1)}, bf16[128,512]{1,0:T(8,128)(2,1)S(1)}, u32[]{:S(2)}, u32[]{:S(2)}) collective-permute-start(bf16[128,512]{1,0:T(8,128)(2,1)S(1)} %add_convert_fusion.refs_4_), channel_id=1, source_target_pairs={{0,64},{64,128},{128,192},{192,0},{1,65},{65,129},{129,193},{193,1... | collective-permute-start | bytes 393224 | tf_op jit(solution)/shard_map/ppermute | solution.py:132
  211.9 8.3 %collective-permute-start.5 = (bf16[128,512]{1,0:T(8,128)(2,1)}, bf16[128,512]{1,0:T(8,128)(2,1)S(1)}, u32[]{:S(2)}, u32[]{:S(2)}) collective-permute-start(bf16[128,512]{1,0:T(8,128)(2,1)} %reduce-scatter.2.cloned.1.call-done.refs_0_), channel_id=1, source_target_pairs={{0,192},{64,0},{128,64},{192,128},{1,193},{65,1},{129,65},{193,129... | collective-permute-start | bytes 393224 | tf_op jit(solution)/shard_map/ppermute | solution.py:132
  215.9 9.9 %collective-permute-start.4 = (bf16[128,512]{1,0:T(8,128)(2,1)}, bf16[128,512]{1,0:T(8,128)(2,1)S(1)}, u32[]{:S(2)}, u32[]{:S(2)}) collective-permute-start(bf16[128,512]{1,0:T(8,128)(2,1)} %reduce-scatter.2.cloned.1.call-done.refs_0_), channel_id=1, source_target_pairs={{0,128},{64,192},{128,0},{192,64},{1,129},{65,193},{129,1},{193,65... | collective-permute-start | bytes 393224 | tf_op jit(solution)/shard_map/ppermute | solution.py:132
  217.1 8.7 %collective-permute-start.3 = (bf16[128,512]{1,0:T(8,128)(2,1)}, bf16[128,512]{1,0:T(8,128)(2,1)S(1)}, u32[]{:S(2)}, u32[]{:S(2)}) collective-permute-start(bf16[128,512]{1,0:T(8,128)(2,1)} %reduce-scatter.2.cloned.1.call-done.refs_0_), channel_id=1, source_target_pairs={{0,64},{64,128},{128,192},{192,0},{1,65},{65,129},{129,193},{193,1... | collective-permute-start | bytes 393224 | tf_op jit(solution)/shard_map/ppermute | solution.py:132
  (6 other events, 10.5 us)
Sparse Core Ops, SparseCore 0:
  10.4 52.1 all-gather.1
  172.1 39.8 reduce-scatter.1
